TPU v7x, 32 devices: a whole 2x2x4 slice. The times are simulated.
32 devices in a mesh: group: 2 (over y), expert: 4 (over z), replica: 2 (over x), learner: 2 (over core).
Axes of the slice: x: 2, y: 2, z: 4, core: 2. Of those that a mesh axis runs over, the one named last changes fastest.
Arguments:
- tokens: bfloat16 [4, 256, 4096], P(None, ('group', 'expert', 'learner')), parts along dimension 1, may hold values from -6 to 6
- gates: float32 [4, 256, 2], P(None, ('group', 'expert', 'learner')), parts along dimension 1, may hold values from 0.05 to 1
- expert_ids: int32 [4, 256, 2], P(None, ('group', 'expert', 'learner')), parts along dimension 1, may hold values from 0 to 3, as said below
- gate_up_tiles: bfloat16 [4, 4096, 2, 1536], P(None, ('expert', 'learner'), None, 'replica'), may hold values from -4 to 4
- gate_up_scales: float32 [4, 32, 2, 12], replicated, may hold values from 0.0078125 to 0.03125
- down_tiles: bfloat16 [4, 1536, 4096], P(None, ('expert', 'learner'), 'replica'), may hold values from -4 to 4
- down_scales: float32 [4, 12, 32], replicated, may hold values from 0.02 to 0.1
Outputs:
- layer_out: bfloat16 [4, 256, 4096], P(None, ('group', 'expert', 'learner'), 'replica'), parts along dimension 1
There are 2 independent parts, one for each index of `group`. A program takes and returns all parts, laid end to end along the dimension named above; an argument that names none is the same for every part. Nothing has to cross between parts.
Inputs may be any that keep to these rules, and one draw needn't show every extreme that they name: `expert_ids`: each row names 2 different experts. Within the rows of one device in one micro-batch (aligned blocks of 16 rows), no expert is named by more than 12 rows; in every micro-batch some expert is named by exactly 12 rows of every device.
All inputs are finite; a program needn't handle non-finite values.
Results may differ from a plain program's by a relative error of at most 0.0076.
Values may be sent and summed in bfloat16 or wider, within the bound.
A program may use at most 128 MiB of HBM per device.

v0:
```python
import jax
import jax.numpy as jnp
from jax import lax
from jax.sharding import PartitionSpec as P


def column_onehot(first_col, count, tile_size, n_blocks):
    block_of = (first_col + jnp.arange(count, dtype=jnp.int32)) // tile_size
    return (block_of[:, None] == jnp.arange(n_blocks, dtype=jnp.int32)[None, :]).astype(jnp.float32)


def body(tokens, gates, expert_ids, gate_up_tiles, gate_up_scales, down_tiles, down_scales):
    step_count, row_count, model_width = tokens.shape
    top_count = expert_ids.shape[2]
    n_expert = lax.axis_size("expert")
    n_learner = lax.axis_size("learner")
    owner_index = lax.axis_index("expert")
    column_part = lax.axis_index("replica")
    local_units = gate_up_tiles.shape[3]
    local_cols = down_tiles.shape[2]
    hidden_width = down_tiles.shape[1] * n_expert * n_learner
    tile_size = model_width // gate_up_scales.shape[1]
    halves_gate_up, halves_down = (
        lax.all_gather(gate_up_tiles, "learner", axis=1, tiled=True),
        lax.all_gather(down_tiles, "learner", axis=1, tiled=True),
    )
    raw_gate_up, raw_down = (
        lax.all_to_all(halves_gate_up, "expert", split_axis=0, concat_axis=1, tiled=True),
        lax.all_to_all(halves_down, "expert", split_axis=0, concat_axis=1, tiled=True),
    )
    scales_gate_up = lax.dynamic_index_in_dim(gate_up_scales, owner_index, 0, keepdims=False)
    onehot_units = column_onehot(
        column_part * local_units, local_units, tile_size, scales_gate_up.shape[2]
    )
    unit_scale = jnp.einsum(
        "bgc,fc->bgf", scales_gate_up, onehot_units, precision=lax.Precision.HIGHEST
    )
    expanded = (
        raw_gate_up[0]
        .astype(jnp.float32)
        .reshape(scales_gate_up.shape[0], tile_size, 2, local_units)
    )
    w_gate_up = (
        (expanded * unit_scale[:, None]).astype(jnp.bfloat16).reshape(model_width, 2 * local_units)
    )
    scales_down = lax.dynamic_index_in_dim(down_scales, owner_index, 0, keepdims=False)
    onehot_cols = column_onehot(
        column_part * local_cols, local_cols, tile_size, scales_down.shape[1]
    )
    col_scale = jnp.einsum("fb,db->fd", scales_down, onehot_cols, precision=lax.Precision.HIGHEST)
    expanded_down = (
        raw_down[0].astype(jnp.float32).reshape(scales_down.shape[0], tile_size, local_cols)
    )
    w_down = (
        (expanded_down * col_scale[:, None]).astype(jnp.bfloat16).reshape(hidden_width, local_cols)
    )
    gate_share = gates / jnp.sum(gates, axis=2, keepdims=True)
    capacity = row_count * top_count // (n_expert - 1) + 2

    def expert_rows(received):
        slot_count = received.shape[1]
        flat_rows = received.reshape(-1, model_width)
        gate_up_out = jnp.dot(flat_rows, w_gate_up, preferred_element_type=jnp.float32)
        hidden = (jax.nn.silu(gate_up_out[:, :local_units]) * gate_up_out[:, local_units:]).astype(
            jnp.bfloat16
        )
        summed = jnp.dot(
            lax.all_gather(hidden, "replica", axis=1, tiled=True),
            w_down,
            preferred_element_type=jnp.float32,
        )
        result = summed.astype(jnp.bfloat16).reshape(n_expert, slot_count, local_cols)
        return lax.all_to_all(result, "expert", split_axis=0, concat_axis=0, tiled=True)

    def serve(block_tokens, block_ids, block_share, slot_total):
        experts = jnp.arange(n_expert, dtype=jnp.int32)
        picked = block_ids[:, :, None] == experts[None, None, :]
        chosen = jnp.sum(picked.astype(jnp.int32), axis=1)
        weight = jnp.sum(jnp.where(picked, block_share[:, :, None], 0.0), axis=1)
        row_rank = jnp.cumsum(chosen, axis=0) - chosen
        slot_ids = jnp.arange(slot_total, dtype=jnp.int32)
        placement = (chosen.T[:, None, :] == 1) & (
            row_rank.T[:, None, :] == slot_ids[None, :, None]
        )
        sending = jnp.einsum(
            "jcn,nd->jcd",
            placement.astype(jnp.bfloat16),
            block_tokens,
            preferred_element_type=jnp.float32,
        ).astype(jnp.bfloat16)
        returned = expert_rows(
            lax.all_to_all(sending, "expert", split_axis=0, concat_axis=0, tiled=True)
        )
        combine_weight = placement.astype(jnp.float32) * weight.T[:, None, :]
        blended = jnp.einsum(
            "jcn,jcd->nd",
            combine_weight,
            returned.astype(jnp.float32),
            precision=lax.Precision.HIGHEST,
        )
        return blended.astype(jnp.bfloat16)

    per_batch = [
        serve(tokens[batch_index], expert_ids[batch_index], gate_share[batch_index], capacity)
        for batch_index in range(step_count)
    ]
    layer_out = jnp.stack(per_batch)
    return layer_out


def solution(mesh):
    placed = (
        P(None, ("group", "expert", "learner"), None),
        P(None, ("group", "expert", "learner"), None),
        P(None, ("group", "expert", "learner"), None),
        P(None, ("expert", "learner"), None, "replica"),
        P(),
        P(None, ("expert", "learner"), "replica"),
        P(),
    )
    return jax.shard_map(
        body,
        mesh=mesh,
        in_specs=placed,
        out_specs=P(None, ("group", "expert", "learner"), "replica"),
        check_vma=False,
    )
```

profile of v0, /device:TPU:0, one launch (start us, length us, event | category | flops | bytes accessed | tf_op | source)
XLA Modules:
  0.0 616.4 jit_solution(12386967303056879291)
XLA Ops:
  11.1 6.3 %all-to-all-start.8 = ((bf16[4,12,4096]{2,1,0:T(8,128)(2,1)}), bf16[4,12,4096]{2,1,0:T(8,128)(2,1)S(1)}, u32[]{:S(2)}, u32[]{:S(2)}) async-start(bf16[4,12,4096]{2,1,0:T(8,128)(2,1)} %convolution_convert_fusion), calls=%async_computation.8 | async-start | bytes 1048576 | tf_op jit(solution)/shard_map/all_to_all | solution.py:92
  17.8 2.2 convolution_convert_fusion.1
  19.9 12.0 %all-to-all-done.8 = bf16[4,12,4096]{2,1,0:T(8,128)(2,1)S(1)} async-done(((bf16[4,12,4096]{2,1,0:T(8,128)(2,1)}), bf16[4,12,4096]{2,1,0:T(8,128)(2,1)S(1)}, u32[]{:S(2)}, u32[]{:S(2)}) %all-to-all-start.8) | async-done | bytes 393248 | tf_op jit(solution)/shard_map/all_to_all | solution.py:92
  31.9 3.5 all-to-all-start.6
  36.8 12.5 %all-to-all-done.6 = bf16[4,12,4096]{2,1,0:T(8,128)(2,1)S(1)} async-done(((bf16[4,12,4096]{2,1,0:T(8,128)(2,1)}), bf16[4,12,4096]{2,1,0:T(8,128)(2,1)S(1)}, u32[]{:S(2)}, u32[]{:S(2)}) %all-to-all-start.6) | async-done | bytes 393248 | tf_op jit(solution)/shard_map/all_to_all | solution.py:92
  49.4 3.5 all-to-all-start.4
  53.3 13.4 %all-to-all-done.4 = bf16[4,12,4096]{2,1,0:T(8,128)(2,1)S(1)} async-done(((bf16[4,12,4096]{2,1,0:T(8,128)(2,1)}), bf16[4,12,4096]{2,1,0:T(8,128)(2,1)S(1)}, u32[]{:S(2)}, u32[]{:S(2)}) %all-to-all-start.4) | async-done | bytes 393248 | tf_op jit(solution)/shard_map/all_to_all | solution.py:92
  66.8 16.4 %all_to_all.58 = bf16[4,12,4096]{2,1,0:T(8,128)(2,1)S(1)} all-to-all(bf16[4,12,4096]{2,1,0:T(8,128)(2,1)S(1)} %convolution_convert_fusion.3), channel_id=1, replica_groups=mesh['group'=2,'expert'=4,'replica'=2,'learner'=2] {'expert'}, dimensions={0} | all-to-all | bytes 786432 | tf_op jit(solution)/shard_map/all_to_all | solution.py:92
  83.1 5.2 all-to-all-start.2
  88.4 137.2 %all-to-all-done.2 = bf16[4,384,2048]{2,1,0:T(8,128)(2,1)} async-done(((bf16[4,384,2048]{2,1,0:T(8,128)(2,1)}), bf16[4,384,2048]{2,1,0:T(8,128)(2,1)}, u32[]{:S(2)}, u32[]{:S(2)}) %all-to-all-start.2) | async-done | bytes 6291488 | tf_op jit(solution)/shard_map/all_to_all | solution.py:29
  225.6 6.3 %all-to-all-start.1 = ((bf16[4,1024,2,768]{3,2,1,0:T(2,128)(2,1)}), bf16[4,1024,2,768]{3,2,1,0:T(2,128)(2,1)}, u32[]{:S(2)}, u32[]{:S(2)}) async-start(bf16[4,1024,2,768]{3,2,1,0:T(2,128)(2,1)} %all-gather.3.cloned.1.call-done), calls=%async_computation.1 | async-start | bytes 25165824 | tf_op jit(solution)/shard_map/all_to_all | solution.py:28
  234.4 7.7 %fusion.1 = bf16[1536,2048]{1,0:T(8,128)(2,1)} fusion(bf16[4,384,2048]{2,1,0:T(8,128)(2,1)} %all-to-all-done.2, f32[12,2048]{1,0:T(8,128)S(1)} %fusion.10), kind=kLoop, calls=%fused_computation.3 | loop fusion | flops 9437184 | bytes 12681216 | tf_op jit(solution)/shard_map/convert_element_type | solution.py:55
  242.2 262.2 %all-to-all-done.1 = bf16[4,1024,2,768]{3,2,1,0:T(2,128)(2,1)} async-done(((bf16[4,1024,2,768]{3,2,1,0:T(2,128)(2,1)}), bf16[4,1024,2,768]{3,2,1,0:T(2,128)(2,1)}, u32[]{:S(2)}, u32[]{:S(2)}) %all-to-all-start.1) | async-done | bytes 12582944 | tf_op jit(solution)/shard_map/all_to_all | solution.py:28
  504.4 11.4 %fusion = bf16[32,128,2,768]{3,2,1,0:T(2,128)(2,1)S(1)} fusion(bf16[32,128,2,768]{3,2,1,0:T(2,128)(2,1)} %bitcast.42, f32[32,2,768]{2,1,0:T(2,128)S(1)} %copy.58), kind=kLoop, calls=%fused_computation.1 | loop fusion | flops 18874368 | bytes 25362432 | tf_op jit(solution)/shard_map/convert_element_type | solution.py:44
  515.8 6.4 %copy.77 = bf16[512,8,2,768]{3,1,2,0:T(8,128)(2,1)S(1)} copy(bf16[512,8,2,768]{3,2,1,0:T(2,128)(2,1)S(1)} %bitcast.133) | data formatting | bytes 25165824
  522.2 5.7 copy-done.2
  527.9 2.2 fusion.83
  530.2 5.0 all_gather.23
  537.2 3.4 all-to-all-start.9
  540.6 6.9 %fusion.82 = f32[48,1536]{1,0:T(8,128)S(1)} fusion(bf16[48,4096]{1,0:T(8,128)(2,1)S(1)} %reshape.156, bf16[4096,1536]{1,0:T(8,128)(2,1)} %bitcast.124), kind=kOutput, calls=%fused_computation.142 | convolution fusion | flops 603979776 | bytes 13271040 | tf_op jit(solution)/shard_map/dot_general | solution.py:63
  547.6 5.2 all_gather.22
  552.8 6.9 %fusion.81 = f32[48,1536]{1,0:T(8,128)S(1)} fusion(bf16[48,4096]{1,0:T(8,128)(2,1)S(1)} %reshape.154, bf16[4096,1536]{1,0:T(8,128)(2,1)} %bitcast.125), kind=kOutput, calls=%fused_computation.141 | convolution fusion | flops 603979776 | bytes 13271040 | tf_op jit(solution)/shard_map/dot_general | solution.py:63
  559.8 2.2 fusion.80
  564.1 5.0 all_gather.21
  569.1 5.0 all-to-all-start.7
  574.1 4.0 convolution_convert_fusion.6
  578.9 5.0 all_gather.19
  584.0 5.1 all-to-all-start.5
  589.1 4.0 convolution_convert_fusion.7
  593.8 2.2 all-to-all-done.5
  596.0 5.5 all-to-all-start.3
  603.0 5.3 all-to-all-done.3
  (109 shorter events, 17.7 us)
Async XLA Ops:
  6.5 225.4 %copy-start = (f32[4,32,2,12]{1,2,3,0:T(2,128)S(1)}, f32[4,32,2,12]{1,2,3,0:T(2,128)}, u32[]{:S(2)}) copy-start(f32[4,32,2,12]{1,2,3,0:T(2,128)} %param.11) | copy-start | bytes 36868
  6.5 29.1 %copy-start.3 = (bf16[4,16,4096]{2,1,0:T(8,128)(2,1)S(1)}, bf16[4,16,4096]{2,1,0:T(8,128)(2,1)}, u32[]{:S(2)}) copy-start(bf16[4,16,4096]{2,1,0:T(8,128)(2,1)} %param.7) | copy-start | bytes 1572868
  6.5 76.6 %all-gather.5.cloned.1.call-start = ((), (), s32[]{:S(2)}) async-start(), calls=%async_computation.11 | async-start | bytes 9437184 | tf_op jit(solution)/shard_map/all_gather | solution.py:25
  7.3 81.2 %all-gather.3.cloned.1.call-start = ((), (), s32[]{:S(2)}) async-start(), calls=%async_computation.10 | async-start | bytes 18874368 | tf_op jit(solution)/shard_map/all_gather | solution.py:24
  9.0 216.6 %copy-start.5 = (pred[4,16]{1,0:T(4,128)(4,1)}, pred[4,16]{1,0:T(4,128)(4,1)S(1)}, u32[]{:S(2)}) copy-start(pred[4,16]{1,0:T(4,128)(4,1)S(1)} %compare_bitcast_fusion) | copy-start | bytes 196
  11.1 20.8 %all-to-all-start.8 = ((bf16[4,12,4096]{2,1,0:T(8,128)(2,1)}), bf16[4,12,4096]{2,1,0:T(8,128)(2,1)S(1)}, u32[]{:S(2)}, u32[]{:S(2)}) async-start(bf16[4,12,4096]{2,1,0:T(8,128)(2,1)} %convolution_convert_fusion), calls=%async_computation.8 | async-start | bytes 1048576 | tf_op jit(solution)/shard_map/all_to_all | solution.py:92
  17.8 14.1 %copy-start.7 = (pred[4,16]{1,0:T(4,128)(4,1)}, pred[4,16]{1,0:T(4,128)(4,1)S(1)}, u32[]{:S(2)}) copy-start(pred[4,16]{1,0:T(4,128)(4,1)S(1)} %compare_bitcast_fusion.1) | copy-start | bytes 196
  31.9 17.4 %all-to-all-start.6 = ((bf16[4,12,4096]{2,1,0:T(8,128)(2,1)}), bf16[4,12,4096]{2,1,0:T(8,128)(2,1)S(1)}, u32[]{:S(2)}, u32[]{:S(2)}) async-start(bf16[4,12,4096]{2,1,0:T(8,128)(2,1)} %convolution_convert_fusion.1), calls=%async_computation.6 | async-start | bytes 1048576 | tf_op jit(solution)/shard_map/all_to_all | solution.py:92
  35.6 17.3 %copy-start.9 = (pred[4,16]{1,0:T(4,128)(4,1)}, pred[4,16]{1,0:T(4,128)(4,1)S(1)}, u32[]{:S(2)}) copy-start(pred[4,16]{1,0:T(4,128)(4,1)S(1)} %compare_bitcast_fusion.2) | copy-start | bytes 196
  49.4 17.4 %all-to-all-start.4 = ((bf16[4,12,4096]{2,1,0:T(8,128)(2,1)}), bf16[4,12,4096]{2,1,0:T(8,128)(2,1)S(1)}, u32[]{:S(2)}, u32[]{:S(2)}) async-start(bf16[4,12,4096]{2,1,0:T(8,128)(2,1)} %convolution_convert_fusion.2), calls=%async_computation.4 | async-start | bytes 1048576 | tf_op jit(solution)/shard_map/all_to_all | solution.py:92
  52.9 172.7 %copy-start.11 = (pred[4,16]{1,0:T(4,128)(4,1)}, pred[4,16]{1,0:T(4,128)(4,1)S(1)}, u32[]{:S(2)}) copy-start(pred[4,16]{1,0:T(4,128)(4,1)S(1)} %compare_bitcast_fusion.3) | copy-start | bytes 196
  83.1 142.4 %all-to-all-start.2 = ((bf16[4,384,2048]{2,1,0:T(8,128)(2,1)}), bf16[4,384,2048]{2,1,0:T(8,128)(2,1)}, u32[]{:S(2)}, u32[]{:S(2)}) async-start(bf16[4,384,2048]{2,1,0:T(8,128)(2,1)} %all-gather.5.cloned.1.call-done), calls=%async_computation.2 | async-start | bytes 12582912 | tf_op jit(solution)/shard_map/all_to_all | solution.py:29
  88.4 144.0 %copy-start.4 = (f32[4,16,2]{1,2,0:T(2,128)S(1)}, f32[4,16,2]{1,2,0:T(2,128)}, u32[]{:S(2)}) copy-start(f32[4,16,2]{1,2,0:T(2,128)} %param.8) | copy-start | bytes 1540
  225.6 278.8 %all-to-all-start.1 = ((bf16[4,1024,2,768]{3,2,1,0:T(2,128)(2,1)}), bf16[4,1024,2,768]{3,2,1,0:T(2,128)(2,1)}, u32[]{:S(2)}, u32[]{:S(2)}) async-start(bf16[4,1024,2,768]{3,2,1,0:T(2,128)(2,1)} %all-gather.3.cloned.1.call-done), calls=%async_computation.1 | async-start | bytes 25165824 | tf_op jit(solution)/shard_map/all_to_all | solution.py:28
  522.2 5.7 copy-start.2
  522.2 13.0 %slice-start.3 = ((s8[6291456]{0:T(1024)(128)(4,1)}), s8[4194304]{0:T(1024)(128)(4,1)S(1)}, s32[]{:S(2)}) async-start(s8[6291456]{0:T(1024)(128)(4,1)} %bitcast.129), calls=%async_computation.15 | async-start | bytes 8388608
  527.9 7.3 %slice-start.4 = ((s8[6291456]{0:T(1024)(128)(4,1)}), s8[2097152]{0:T(1024)(128)(4,1)S(1)}, s32[]{:S(2)}) async-start(s8[6291456]{0:T(1024)(128)(4,1)} %bitcast.129), calls=%async_computation.16 | async-start | bytes 4194304
  537.2 31.9 %all-to-all-start.9 = ((bf16[4,12,2048]{2,1,0:T(8,128)(2,1)}), bf16[4,12,2048]{2,1,0:T(8,128)(2,1)S(1)}, u32[]{:S(2)}, u32[]{:S(2)}) async-start(bf16[4,12,2048]{2,1,0:T(8,128)(2,1)} %reshape.159), calls=%async_computation.9 | async-start | bytes 524288 | tf_op jit(solution)/shard_map/all_to_all | solution.py:73
  540.6 19.1 %slice-start = ((s8[12582912]{0:T(1024)(128)(4,1)}), s8[4194304]{0:T(1024)(128)(4,1)S(1)}, s32[]{:S(2)}) async-start(s8[12582912]{0:T(1024)(128)(4,1)} %bitcast.126), calls=%async_computation.12 | async-start | bytes 8388608
  540.6 19.1 %slice-start.1 = ((s8[12582912]{0:T(1024)(128)(4,1)}), s8[4194304]{0:T(1024)(128)(4,1)S(1)}, s32[]{:S(2)}) async-start(s8[12582912]{0:T(1024)(128)(4,1)} %bitcast.126), calls=%async_computation.13 | async-start | bytes 8388608
  552.8 6.9 %slice-start.2 = ((s8[12582912]{0:T(1024)(128)(4,1)}), s8[4194304]{0:T(1024)(128)(4,1)S(1)}, s32[]{:S(2)}) async-start(s8[12582912]{0:T(1024)(128)(4,1)} %bitcast.126), calls=%async_computation.14 | async-start | bytes 8388608
  552.8 9.2 %slice-start.5 = ((s8[6291456]{0:T(1024)(128)(4,1)}), s8[4194304]{0:T(1024)(128)(4,1)S(1)}, s32[]{:S(2)}) async-start(s8[6291456]{0:T(1024)(128)(4,1)} %bitcast.131), calls=%async_computation.17 | async-start | bytes 8388608
  559.8 2.2 slice-start.6
  559.8 49.8 %copy-start.1 = (f32[4,32,2,12]{1,2,3,0:T(2,128)S(1)}, f32[4,32,2,12]{1,2,3,0:T(2,128)}, u32[]{:S(2)}) copy-start(f32[4,32,2,12]{1,2,3,0:T(2,128)} %param.11) | copy-start | bytes 36868
  562.0 39.5 %copy-start.6 = (pred[4,16]{1,0:T(4,128)(4,1)S(1)}, pred[4,16]{1,0:T(4,128)(4,1)}, u32[]{:S(2)}) copy-start(pred[4,16]{1,0:T(4,128)(4,1)} %copy-done.5) | copy-start | bytes 196
  562.0 40.0 %copy-start.8 = (pred[4,16]{1,0:T(4,128)(4,1)S(1)}, pred[4,16]{1,0:T(4,128)(4,1)}, u32[]{:S(2)}) copy-start(pred[4,16]{1,0:T(4,128)(4,1)} %copy-done.7) | copy-start | bytes 196
  562.0 40.5 %copy-start.10 = (pred[4,16]{1,0:T(4,128)(4,1)S(1)}, pred[4,16]{1,0:T(4,128)(4,1)}, u32[]{:S(2)}) copy-start(pred[4,16]{1,0:T(4,128)(4,1)} %copy-done.9) | copy-start | bytes 196
  562.0 46.2 %copy-start.12 = (pred[4,16]{1,0:T(4,128)(4,1)S(1)}, pred[4,16]{1,0:T(4,128)(4,1)}, u32[]{:S(2)}) copy-start(pred[4,16]{1,0:T(4,128)(4,1)} %copy-done.11) | copy-start | bytes 196
  569.1 14.9 %all-to-all-start.7 = ((bf16[4,12,2048]{2,1,0:T(8,128)(2,1)}), bf16[4,12,2048]{2,1,0:T(8,128)(2,1)S(1)}, u32[]{:S(2)}, u32[]{:S(2)}) async-start(bf16[4,12,2048]{2,1,0:T(8,128)(2,1)} %reshape.157), calls=%async_computation.7 | async-start | bytes 524288 | tf_op jit(solution)/shard_map/all_to_all | solution.py:73
  584.0 12.0 %all-to-all-start.5 = ((bf16[4,12,2048]{2,1,0:T(8,128)(2,1)}), bf16[4,12,2048]{2,1,0:T(8,128)(2,1)S(1)}, u32[]{:S(2)}, u32[]{:S(2)}) async-start(bf16[4,12,2048]{2,1,0:T(8,128)(2,1)} %reshape.155), calls=%async_computation.5 | async-start | bytes 524288 | tf_op jit(solution)/shard_map/all_to_all | solution.py:73
  596.0 12.3 %all-to-all-start.3 = ((bf16[4,12,2048]{2,1,0:T(8,128)(2,1)}), bf16[4,12,2048]{2,1,0:T(8,128)(2,1)S(1)}, u32[]{:S(2)}, u32[]{:S(2)}) async-start(bf16[4,12,2048]{2,1,0:T(8,128)(2,1)} %reshape.153), calls=%async_computation.3 | async-start | bytes 524288 | tf_op jit(solution)/shard_map/all_to_all | solution.py:73
Sparse Core Ops, SparseCore 0:
  8.9 19.4 all-gather.4
  30.0 25.6 all-gather.2
where the time goes:
time: 617 us; the launch traced here: 616 us
  waiting for transfers between devices  446 us (72%)
  starting transfers between devices  43.9 us (7%)
  matrix products  37.5 us (6%)
  blocking collectives  36.7 us (6%)
  other arithmetic  20.4 us (3%)
  local copies, waits for them, and re-layouts  17.9 us (3%)
  between operations  13.9 us (2%)
    all_to_all x1, waiting for transfers between devices, body(): lax.all_to_all(halves_gate_up, 'expert', split_axis=0, concat_axis=1, til...  262 us
    all_to_all x1, waiting for transfers between devices, body(): lax.all_to_all(halves_down, 'expert', split_axis=0, concat_axis=1, tiled=...  137 us
    all_to_all x3, waiting for transfers between devices, serve(): lax.all_to_all(sending, 'expert', split_axis=0, concat_axis=0, tiled=True)  37.9 us
    all_gather x4, blocking collectives, expert_rows(): lax.all_gather(hidden, 'replica', axis=1, tiled=True)  20.3 us
    all_to_all x4, starting transfers between devices, expert_rows(): lax.all_to_all(result, 'expert', split_axis=0, concat_axis=0, tiled=True)  19.1 us
    dot_general x4, matrix products, expert_rows(): jnp.dot(flat_rows, w_gate_up, preferred_element_type=jnp.float32)  18.2 us
    all_to_all x1, blocking collectives, serve(): lax.all_to_all(sending, 'expert', split_axis=0, concat_axis=0, tiled=True)  16.4 us
    all_to_all x3, starting transfers between devices, serve(): lax.all_to_all(sending, 'expert', split_axis=0, concat_axis=0, tiled=True)  13.3 us
  transfers between devices with their start and end apart: 11, of which 7 were waited for; matrix products, arithmetic and copies ran while one was open for 8% of the time, Pallas kernels for 0%

commit v1 on v0

v1 whole, which is shorter than its diff:
```python
import jax
import jax.numpy as jnp
from jax import lax
from jax.sharding import PartitionSpec as P

ROW_AXES = ("expert", "learner")


def body(tokens, gates, expert_ids, gate_up_tiles, gate_up_scales, down_tiles, down_scales):
    steps, rows_dev, width = tokens.shape
    top = expert_ids.shape[2]
    n_z = lax.axis_size("expert")
    n_c = lax.axis_size("learner")
    n_x = lax.axis_size("replica")
    n_dev = n_z * n_c
    z, c, x = lax.axis_index("expert"), lax.axis_index("learner"), lax.axis_index("replica")
    me = z * n_c + c
    experts, d_loc, _, units = gate_up_tiles.shape
    f_loc, cols = down_tiles.shape[1:]
    tile = width // gate_up_scales.shape[1]
    piece = units // n_dev
    f32, bf16 = jnp.float32, jnp.bfloat16

    xs = lax.all_to_all(tokens, ROW_AXES, split_axis=2, concat_axis=1, tiled=True)
    n_rows = steps * rows_dev * n_dev
    xs = xs.reshape(n_rows, d_loc)
    share = gates / jnp.sum(gates, axis=2, keepdims=True)
    route = jnp.concatenate([expert_ids.astype(f32), share], axis=2)
    route = lax.all_gather(route, ROW_AXES, axis=1, tiled=True).reshape(n_rows, 2 * top)
    ids = route[:, :top].T.astype(jnp.int32)
    share = route[:, top:].T

    def take(scales, axis, first, count):
        index = (first + jnp.arange(count)) // tile
        onehot = (index[:, None] == jnp.arange(scales.shape[axis])[None, :]).astype(f32)
        return jnp.moveaxis(
            jnp.tensordot(scales, onehot, axes=([axis], [1]), precision=lax.Precision.HIGHEST), -1, axis
        )

    s1 = take(take(gate_up_scales, 1, me * d_loc, d_loc), 3, x * units, units)
    w1 = (gate_up_tiles.astype(f32) * s1).astype(bf16).reshape(experts * d_loc, 2 * units)
    s2 = take(take(down_scales, 1, me * f_loc, f_loc), 2, x * cols, cols)
    w2 = (down_tiles.astype(f32) * s2).astype(bf16).reshape(experts * f_loc, cols)

    names = jnp.arange(experts, dtype=jnp.int32)
    picked = ids[:, :, None] == names
    masked = jnp.where(picked[..., None], xs[None, :, None, :], jnp.zeros((), bf16))
    part = jnp.dot(masked.reshape(top * n_rows, experts * d_loc), w1, preferred_element_type=f32)
    part = part.astype(bf16).reshape(top * n_rows, 2, n_z, n_c, piece)

    def core_sum(value, axis):
        mine = lax.dynamic_index_in_dim(value, c, axis, keepdims=False)
        other = lax.dynamic_index_in_dim(value, 1 - c, axis, keepdims=False)
        got = lax.ppermute(other, "learner", [(0, 1), (1, 0)])
        return (mine.astype(f32) + got.astype(f32)).astype(bf16)

    half = jnp.moveaxis(core_sum(part, 3), 2, 0)
    got = lax.all_to_all(half, "expert", split_axis=0, concat_axis=0, tiled=True)
    total = jnp.sum(got.astype(f32), axis=0)
    hidden = jax.nn.silu(total[:, 0]) * total[:, 1]
    hidden = (hidden * share.reshape(-1)[:, None]).astype(bf16)

    pieces = []
    for turn in range(n_x):
        pairs = []
        for zz in range(n_z):
            for xx in range(n_x):
                for cc in range(n_c):
                    q = zz * n_c + cc
                    owner = (n_dev // n_x) * xx + q // n_x
                    source = (zz * n_x + xx) * n_c + cc
                    target = (owner // n_c * n_x + (q + turn) % n_x) * n_c + owner % n_c
                    pairs.append((source, target))
        pieces.append(lax.ppermute(hidden, ("expert", "replica", "learner"), pairs))
    stack = jnp.stack(pieces)
    order = jnp.mod(x - jnp.arange(n_x), n_x)
    ordered = jnp.take(stack, order, axis=0)
    h = jnp.moveaxis(ordered, 0, 1).reshape(top, n_rows, f_loc)
    wide = jnp.zeros((n_rows, experts, f_loc), bf16)
    for k in range(top):
        wide = wide + jnp.where(picked[k][..., None], h[k][:, None, :], jnp.zeros((), bf16))
    out = jnp.dot(wide.reshape(n_rows, experts * f_loc), w2, preferred_element_type=f32)
    out = out.astype(bf16).reshape(steps, n_z, n_c, rows_dev, cols)
    half = jnp.moveaxis(core_sum(out, 2), 1, 0)
    got = lax.all_to_all(half, "expert", split_axis=0, concat_axis=0, tiled=True)
    return jnp.sum(got.astype(f32), axis=0).astype(bf16)


def solution(mesh):
    placed = (
        P(None, ("group", "expert", "learner"), None),
        P(None, ("group", "expert", "learner"), None),
        P(None, ("group", "expert", "learner"), None),
        P(None, ("expert", "learner"), None, "replica"),
        P(),
        P(None, ("expert", "learner"), "replica"),
        P(),
    )
    return jax.shard_map(
        body,
        mesh=mesh,
        in_specs=placed,
        out_specs=P(None, ("group", "expert", "learner"), "replica"),
        check_vma=False,
    )
```

time: 617 us -> 198 us (0.32)
  waiting for transfers between devices: 446 us -> 45.7 us
  local copies, waits for them, and re-layouts: 17.9 us -> 48.4 us
  starting transfers between devices: 43.9 us -> 15.6 us
  blocking collectives: 36.7 us -> 50.9 us
  between operations: 13.9 us -> 0.3 us
  matrix products: 37.5 us -> 25.9 us
  other arithmetic: 20.4 us -> 10 us
    all_to_all x9 -> x2, waiting for transfers between devices: 445 us -> 31.5 us  [the longest x1 31.5 us: body(): lax.all_to_all(half, 'expert', split_axis=0, concat_axis=0, tiled=True)]
    all_to_all x9 -> x2, starting transfers between devices: 43.9 us -> 10.9 us  [the longest x1 6.33 us: body(): lax.all_to_all(tokens, ROW_AXES, split_axis=2, concat_axis=1, tiled=True)]
    all_to_all x1, blocking collectives: 16.4 us -> 36 us  [body(): lax.all_to_all(half, 'expert', split_axis=0, concat_axis=0, tiled=True)]
    convert_element_type x6 -> x2, other arithmetic: 19.4 us -> 0.13 us  [the longest x1 0.13 us: body(): hidden = (hidden * share.reshape(-1)[:, None]).astype(bf16)]
    convert_element_type x0 -> x2, local copies, waits for them, and re-layouts: none -> 15 us  [the longest x1 11.9 us: body(): (gate_up_tiles.astype(f32) * s1).astype(bf16)]
    ppermute x0 -> x4, waiting for transfers between devices: none -> 14.2 us  [the longest x2 8.48 us: body(): pieces.append(lax.ppermute(hidden, ('expert', 'replica', 'learner'), pairs))]
    dot_general x18 -> x6, matrix products: 37.5 us -> 25.9 us  [the longest x4 15.9 us: take(): jnp.tensordot(scales, onehot, axes=([axis], [1]), precision=lax.Precision...]
    unnamed x41 -> x22, local copies, waits for them, and re-layouts: 12.2 us -> 22 us
  transfers between devices with their start and end apart: 11 -> 6, of which waited for: 7 -> 4; matrix products, arithmetic and copies ran while one was open for 8% -> 16% of each run, Pallas kernels for 0% -> 0%
where the time goes in v1:
time: 198 us; the launch traced here: 197 us
  blocking collectives  50.9 us (26%)
  local copies, waits for them, and re-layouts  48.4 us (24%)
  waiting for transfers between devices  45.7 us (23%)
  matrix products  25.9 us (13%)
  starting transfers between devices  15.6 us (8%)
  other arithmetic  10 us (5%)
    all_to_all x1, blocking collectives, body(): lax.all_to_all(half, 'expert', split_axis=0, concat_axis=0, tiled=True)  36 us
    all_to_all x1, waiting for transfers between devices, body(): lax.all_to_all(half, 'expert', split_axis=0, concat_axis=0, tiled=True)  31.5 us
    unnamed x22, local copies, waits for them, and re-layouts  22 us
    dot_general x4, matrix products, take(): jnp.tensordot(scales, onehot, axes=([axis], [1]), precision=lax.Precision...  15.9 us
    all_gather x1, blocking collectives, body(): lax.all_gather(route, ROW_AXES, axis=1, tiled=True).reshape(n_rows, 2 * top)  14.9 us
    convert_element_type x1, local copies, waits for them, and re-layouts, body(): (gate_up_tiles.astype(f32) * s1).astype(bf16)  11.9 us
    ppermute x2, waiting for transfers between devices, body(): pieces.append(lax.ppermute(hidden, ('expert', 'replica', 'learner'), pairs))  8.48 us
    dot_general x1, matrix products, body(): jnp.dot(masked.reshape(top * n_rows, experts * d_loc), w1, preferred_elem...  8.08 us
  transfers between devices with their start and end apart: 6, of which 4 were waited for; matrix products, arithmetic and copies ran while one was open for 16% of the time, Pallas kernels for 0%

profile of v1, /device:TPU:0, one launch (start us, length us, event | category | flops | bytes accessed | tf_op | source)
XLA Modules:
  0.0 196.8 jit_solution(6525489894100266437)
XLA Ops:
  0.0 5.9 %copy.56 = bf16[4,16,4096]{1,0,2:T(4,128)(2,1)} copy(bf16[4,16,4096]{2,1,0:T(8,128)(2,1)} %param.7) | data formatting | bytes 1048576 | tf_op args[0]
  5.9 6.5 %reshape.198 = bf16[8,2,16384]{2,1,0:T(2,128)(2,1)} reshape(bf16[4096,4,16]{2,1,0:T(4,128)(2,1)} %bitcast.94) | data formatting | bytes 1048576
  12.3 6.3 %all-to-all-start = ((bf16[8,2,16384]{2,1,0:T(2,128)(2,1)}), bf16[8,2,16384]{2,1,0:T(2,128)(2,1)S(1)}, u32[]{:S(2)}, u32[]{:S(2)}) async-start(bf16[8,2,16384]{2,1,0:T(2,128)(2,1)} %reshape.198), calls=%async_computation | async-start | bytes 1048576 | tf_op jit(solution)/shard_map/all_to_all | solution.py:24
  19.0 9.8 %multiply_convert_fusion = bf16[4,512,2,768]{3,1,2,0:T(8,128)(2,1)} fusion(bf16[4,512,2,768]{3,2,1,0:T(2,128)(2,1)} %param.10, f32[4,512,2,12]{1,3,2,0:T(8,128)S(1)} %convolution_bitcast_fusion, s32[768]{0:T(1024)S(1)} %add_select_fusion.1), kind=kOutput, calls=%fused_computation.1 | convolution fusion | flops 462431232 | bytes 12782592 | tf_op jit(solution)/shard_map/dot_general | solution.py:37
  28.7 11.9 %copy.61 = bf16[4,512,2,768]{3,2,1,0:T(2,128)(2,1)S(1)} copy(bf16[4,512,2,768]{3,1,2,0:T(8,128)(2,1)} %multiply_convert_fusion) | data formatting | bytes 12582912 | tf_op jit(solution)/shard_map/convert_element_type | solution.py:41
  40.6 4.0 %copy.73 = bf16[256,8,2,768]{3,1,2,0:T(8,128)(2,1)} copy(bf16[256,8,2,768]{3,2,1,0:T(2,128)(2,1)S(1)} %bitcast.92) | data formatting | bytes 12582912
  44.8 14.9 %all_gather.3 = f32[4,128,4]{2,0,1:T(4,128)S(1)} all-gather(f32[4,16,4]{2,0,1:T(4,128)S(1)} %copy.53), channel_id=1, replica_groups=mesh['group'=2,'expert'=4,'replica'=2,'learner'=2] {'expert','learner'}, dimensions={1}, use_global_device_ids=true | all-gather | bytes 9216 | tf_op jit(solution)/shard_map/all_gather | solution.py:29
  60.2 4.1 %reshape.199 = bf16[4096,4,16]{2,1,0:T(4,128)(2,1)} reshape(bf16[8,2,16384]{2,1,0:T(2,128)(2,1)S(1)} %all-to-all-done) | data formatting | bytes 1048576
  64.3 5.5 %copy.70 = bf16[4,16,8,512]{3,1,2,0:T(8,128)(2,1)S(1)} copy(bf16[4,16,8,512]{1,0,3,2:T(4,128)(2,1)} %bitcast.93) | data formatting | bytes 1048576 | tf_op jit(solution)/shard_map/all_to_all | solution.py:24
  69.8 4.2 %broadcast_select_fusion = bf16[2,512,4,512]{3,2,1,0:T(4,128)(2,1)S(1)} fusion(pred[2,512,4]{2,1,0:T(8,128)(4,1)S(1)} %copy.55, bf16[512,512]{1,0:T(8,128)(2,1)S(1)} %bitcast.102), kind=kLoop, calls=%fused_computation.4 | loop fusion | flops 2097152 | bytes 4722688 | tf_op jit(solution)/shard_map/jit(_where)/select_n | solution.py:47
  74.0 1.4 copy.72
  75.6 8.1 %convolution_convert_fusion = bf16[1024,1536]{1,0:T(8,128)(2,1)} fusion(bf16[1024,2048]{1,0:T(8,128)(2,1)S(1)} %bitcast.101, bf16[2048,1536]{1,0:T(8,128)(2,1)S(1)} %bitcast.100), kind=kOutput, calls=%fused_computation.5 | convolution fusion | flops 6444023808 | bytes 13631488 | tf_op jit(solution)/shard_map/dot_general | solution.py:48
  83.7 3.2 %copy.62 = bf16[1024,1536]{0,1:T(8,128)(2,1)S(1)} copy(bf16[1024,1536]{1,0:T(8,128)(2,1)} %convolution_convert_fusion) | data formatting | bytes 6291456 | tf_op jit(solution)/shard_map/convert_element_type | solution.py:49
  86.8 1.4 dynamic-slice_bitcast_fusion
  88.6 3.4 %collective-permute-done = bf16[1024,2,4,96]{0,3,2,1:T(8,128)(2,1)} collective-permute-done((bf16[1024,2,4,96]{0,3,2,1:T(8,128)(2,1)}, bf16[1024,2,4,96]{0,3,2,1:T(8,128)(2,1)}, u32[]{:S(2)}, u32[]{:S(2)}) %collective-permute-start) | collective-permute-done | bytes 1572896 | tf_op jit(solution)/shard_map/ppermute | solution.py:54
  92.0 2.1 %fusion.2 = bf16[4,1024,2,96]{1,3,0,2:T(8,128)(2,1)S(1)} fusion(bf16[1024,2,4,96]{0,3,2,1:T(8,128)(2,1)} %collective-permute-done, bf16[1024,2,4,2,96]{0,4,3,2,1:T(8,128)(2,1)S(1)} %bitcast.97, s32[]{:T(128)S(6)} %select_n.115), kind=kLoop, calls=%fused_computation.11 | loop fusion | flops 3145728 | bytes 4718596 | tf_op jit(solution)/shard_map/transpose | solution.py:57
  94.1 1.3 copy.63
  95.3 4.6 %all-to-all-start.1 = ((bf16[4,1024,2,96]{1,3,2,0:T(8,128)(2,1)}), bf16[4,1024,2,96]{1,3,2,0:T(8,128)(2,1)S(1)}, u32[]{:S(2)}, u32[]{:S(2)}) async-start(bf16[4,1024,2,96]{1,3,2,0:T(8,128)(2,1)} %copy.63), calls=%async_computation.1 | async-start | bytes 3145728 | tf_op jit(solution)/shard_map/all_to_all | solution.py:58
  100.3 5.6 %multiply_convert_fusion.1 = bf16[4,192,2048]{2,1,0:T(8,128)(2,1)} fusion(bf16[4,192,2048]{2,1,0:T(8,128)(2,1)} %param.12, f32[4,192,32]{1,2,0:T(8,128)S(1)} %convolution_bitcast_fusion.1, s32[2048]{0:T(1024)S(1)} %add_select_fusion), kind=kOutput, calls=%fused_computation.2 | convolution fusion | flops 608763904 | bytes 6397952 | tf_op jit(solution)/shard_map/dot_general | solution.py:37
  105.9 31.5 %all-to-all-done.1 = bf16[4,1024,2,96]{1,3,2,0:T(8,128)(2,1)S(1)} async-done(((bf16[4,1024,2,96]{1,3,2,0:T(8,128)(2,1)}), bf16[4,1024,2,96]{1,3,2,0:T(8,128)(2,1)S(1)}, u32[]{:S(2)}, u32[]{:S(2)}) %all-to-all-start.1) | async-done | bytes 1572896 | tf_op jit(solution)/shard_map/all_to_all | solution.py:58
  137.8 0.8 collective-permute-start.1
  138.6 3.1 %collective-permute-start.2 = (bf16[1024,96]{0,1:T(8,128)(2,1)S(1)}, bf16[1024,96]{0,1:T(8,128)(2,1)S(1)}, u32[]{:S(2)}, u32[]{:S(2)}) collective-permute-start(bf16[1024,96]{0,1:T(8,128)(2,1)S(1)} %fusion.11), channel_id=1, source_target_pairs={{0,2},{1,0},{2,10},{3,8},{4,3},{5,1},{6,11},{7,9},{8,6},{9,4},{10,... | collective-permute-start | bytes 589832 | tf_op jit(solution)/shard_map/ppermute | solution.py:74
  141.8 8.5 %collective-permute-done.2 = bf16[1024,96]{0,1:T(8,128)(2,1)S(1)} collective-permute-done((bf16[1024,96]{0,1:T(8,128)(2,1)S(1)}, bf16[1024,96]{0,1:T(8,128)(2,1)S(1)}, u32[]{:S(2)}, u32[]{:S(2)}) %collective-permute-start.2) | collective-permute-done | bytes 196640 | tf_op jit(solution)/shard_map/ppermute | solution.py:74
  150.3 0.8 pad_maximum_fusion
  151.0 2.3 %gather_fusion = bf16[2,1024,96]{1,2,0:T(8,128)(2,1)} fusion(bf16[2,1024,96]{1,2,0:T(8,128)(2,1)} %pad_maximum_fusion, s32[1024]{0:T(1024)S(1)} %pad_clamp_fusion), kind=kCustom, calls=%fused_computation | custom fusion | bytes 786440 | tf_op jit(solution)/shard_map/jit(_take)/gather | solution.py:77
  153.4 1.1 select_bitcast_fusion
  154.5 1.9 bitcast_convert_fusion
  156.7 0.4 collective-permute-start.3
  157.2 2.3 %collective-permute-done.3 = bf16[4,4,16,2048]{3,2,0,1:T(8,128)(2,1)S(1)} collective-permute-done((bf16[4,4,16,2048]{3,2,0,1:T(8,128)(2,1)S(1)}, bf16[4,4,16,2048]{3,2,0,1:T(8,128)(2,1)S(1)}, u32[]{:S(2)}, u32[]{:S(2)}) %collective-permute-start.3) | collective-permute-done | bytes 1048608 | tf_op jit(solution)/shard_map/ppermute | solution.py:54
  159.5 0.4 fusion.3
  159.9 36.0 %all_to_all.25 = bf16[4,4,16,2048]{3,2,1,0:T(8,128)(2,1)S(1)} all-to-all(bf16[4,4,16,2048]{3,2,1,0:T(8,128)(2,1)S(1)} %fusion.3), channel_id=1, replica_groups=mesh['group'=2,'expert'=4,'replica'=2,'learner'=2] {'expert'}, dimensions={0} | all-to-all | bytes 2097152 | tf_op jit(solution)/shard_map/all_to_all | solution.py:85
  195.8 0.9 reduce_sum.32
  (44 shorter events, 2.4 us)
Async XLA Ops:
  0.0 18.7 %copy-start = (f32[4,32,2,12]{1,2,3,0:T(2,128)S(1)}, f32[4,32,2,12]{1,2,3,0:T(2,128)}, u32[]{:S(2)}) copy-start(f32[4,32,2,12]{1,2,3,0:T(2,128)} %param.11) | copy-start | bytes 36868
  12.3 47.8 %all-to-all-start = ((bf16[8,2,16384]{2,1,0:T(2,128)(2,1)}), bf16[8,2,16384]{2,1,0:T(2,128)(2,1)S(1)}, u32[]{:S(2)}, u32[]{:S(2)}) async-start(bf16[8,2,16384]{2,1,0:T(2,128)(2,1)} %reshape.198), calls=%async_computation | async-start | bytes 1048576 | tf_op jit(solution)/shard_map/all_to_all | solution.py:24
  40.6 4.0 %copy-start.4 = (s32[4,16,2]{1,2,0:T(2,128)S(1)}, s32[4,16,2]{1,2,0:T(2,128)}, u32[]{:S(2)}) copy-start(s32[4,16,2]{1,2,0:T(2,128)} %param.9) | copy-start | bytes 1540
  40.6 4.0 %copy-start.5 = (f32[4,16,2]{1,2,0:T(2,128)S(1)}, f32[4,16,2]{1,2,0:T(2,128)}, u32[]{:S(2)}) copy-start(f32[4,16,2]{1,2,0:T(2,128)} %param.8) | copy-start | bytes 1540
  69.8 5.7 %slice-start = ((s8[6291456]{0:T(1024)(128)(4,1)}), s8[4194304]{0:T(1024)(128)(4,1)S(1)}, s32[]{:S(2)}) async-start(s8[6291456]{0:T(1024)(128)(4,1)} %bitcast.98), calls=%async_computation.3 | async-start | bytes 8388608
  74.0 1.6 slice-start.1
  88.2 3.8 %collective-permute-start = (bf16[1024,2,4,96]{0,3,2,1:T(8,128)(2,1)}, bf16[1024,2,4,96]{0,3,2,1:T(8,128)(2,1)}, u32[]{:S(2)}, u32[]{:S(2)}) collective-permute-start(bf16[1024,2,4,96]{0,3,2,1:T(8,128)(2,1)} %dynamic-slice_bitcast_fusion), channel_id=1, source_target_pairs={{0,1},{1,0},{2,3},{3,2},{4,5},{5,4},{6,7},{7,6},{8,9},{9,8},{10,11... | collective-permute-start | bytes 4718600 | tf_op jit(solution)/shard_map/ppermute | solution.py:54
  94.0 6.0 %copy-start.3 = (f32[4,12,32]{2,0,1:T(4,128)S(1)}, f32[4,12,32]{2,0,1:T(4,128)}, u32[]{:S(2)}) copy-start(f32[4,12,32]{2,0,1:T(4,128)} %param.13) | copy-start | bytes 18436
  95.3 42.0 %all-to-all-start.1 = ((bf16[4,1024,2,96]{1,3,2,0:T(8,128)(2,1)}), bf16[4,1024,2,96]{1,3,2,0:T(8,128)(2,1)S(1)}, u32[]{:S(2)}, u32[]{:S(2)}) async-start(bf16[4,1024,2,96]{1,3,2,0:T(8,128)(2,1)} %copy.63), calls=%async_computation.1 | async-start | bytes 3145728 | tf_op jit(solution)/shard_map/all_to_all | solution.py:58
  137.7 16.8 %copy-start.2 = (bf16[4,192,2048]{2,1,0:T(8,128)(2,1)S(1)}, bf16[4,192,2048]{2,1,0:T(8,128)(2,1)}, u32[]{:S(2)}) copy-start(bf16[4,192,2048]{2,1,0:T(8,128)(2,1)} %multiply_convert_fusion.1) | copy-start | bytes 9437188
  137.8 4.0 %collective-permute-start.1 = (bf16[1024,96]{0,1:T(8,128)(2,1)S(1)}, bf16[1024,96]{0,1:T(8,128)(2,1)S(1)}, u32[]{:S(2)}, u32[]{:S(2)}) collective-permute-start(bf16[1024,96]{0,1:T(8,128)(2,1)S(1)} %fusion.11), channel_id=1, source_target_pairs={{0,0},{1,2},{2,8},{3,10},{4,1},{5,3},{6,9},{7,11},{8,4},{9,6},{10,... | collective-permute-start | bytes 589832 | tf_op jit(solution)/shard_map/ppermute | solution.py:74
  138.6 11.6 %collective-permute-start.2 = (bf16[1024,96]{0,1:T(8,128)(2,1)S(1)}, bf16[1024,96]{0,1:T(8,128)(2,1)S(1)}, u32[]{:S(2)}, u32[]{:S(2)}) collective-permute-start(bf16[1024,96]{0,1:T(8,128)(2,1)S(1)} %fusion.11), channel_id=1, source_target_pairs={{0,2},{1,0},{2,10},{3,8},{4,3},{5,1},{6,11},{7,9},{8,6},{9,4},{10,... | collective-permute-start | bytes 589832 | tf_op jit(solution)/shard_map/ppermute | solution.py:74
  156.7 2.7 %collective-permute-start.3 = (bf16[4,4,16,2048]{3,2,0,1:T(8,128)(2,1)S(1)}, bf16[4,4,16,2048]{3,2,0,1:T(8,128)(2,1)S(1)}, u32[]{:S(2)}, u32[]{:S(2)}) collective-permute-start(bf16[4,4,16,2048]{3,2,0,1:T(8,128)(2,1)S(1)} %bitcast.104), channel_id=1, source_target_pairs={{0,1},{1,0},{2,3},{3,2},{4,5},{5,4},{6,7},{7,6},{8,9},{9,8},{10,11... | collective-permute-start | bytes 3145736 | tf_op jit(solution)/shard_map/ppermute | solution.py:54
  159.5 37.3 %copy-start.1 = (f32[4,32,2,12]{1,2,3,0:T(2,128)S(1)}, f32[4,32,2,12]{1,2,3,0:T(2,128)}, u32[]{:S(2)}) copy-start(f32[4,32,2,12]{1,2,3,0:T(2,128)} %param.11) | copy-start | bytes 36868

commit v2 on v1

--- a/solution.py
+++ b/solution.py
@@ -1,47 +1,277 @@
+import functools
+
 import jax
 import jax.numpy as jnp
 from jax import lax
+from jax.experimental import pallas as pl
+from jax.experimental.pallas import tpu as pltpu
 from jax.sharding import PartitionSpec as P
 
 ROW_AXES = ("expert", "learner")
-
-
-def body(tokens, gates, expert_ids, gate_up_tiles, gate_up_scales, down_tiles, down_scales):
-    steps, rows_dev, width = tokens.shape
-    top = expert_ids.shape[2]
-    n_z = lax.axis_size("expert")
-    n_c = lax.axis_size("learner")
-    n_x = lax.axis_size("replica")
-    n_dev = n_z * n_c
+LANE = 128
+OUT_COLS = 512
+
+
+def shift(index, by, count):
+    return lax.rem(index + by, count)
+
+
+def kernel(sizes, xs, route, w1, w2, out, xm, s_send, s_recv, own, z_send, z_recv, hid, h_recv,
+           wide, q_send, q_recv, q_own, o_send, o_recv,
+           s_ss, s_rs, z_ss, z_rs, h_ss, h_rs, q_ss, q_rs, o_ss, o_rs):
+    n_z, n_x, top, experts, rows, d_loc, f_loc, span = sizes
+    n_c = 2
+    f32, bf16 = jnp.float32, jnp.bfloat16
     z, c, x = lax.axis_index("expert"), lax.axis_index("learner"), lax.axis_index("replica")
     me = z * n_c + c
-    experts, d_loc, _, units = gate_up_tiles.shape
-    f_loc, cols = down_tiles.shape[1:]
-    tile = width // gate_up_scales.shape[1]
+    chunks = w1.shape[0]
+    slots = top * rows
+    per_plane = n_z * n_c // n_x
+    sibling = {"learner": 1 - c}
+
+    def remote(src, dst, send, recv, device):
+        return pltpu.make_async_remote_copy(
+            src_ref=src, dst_ref=dst, send_sem=send, recv_sem=recv,
+            device_id=device, device_id_type=pl.DeviceIdType.MESH)
+
+    barrier = pltpu.get_barrier_semaphore()
+    everyone = n_z * n_c * n_x
+    here = (z * n_x + x) * n_c + c
+    for turn in range(1, everyone):
+        there = shift(here, turn, everyone)
+        pl.semaphore_signal(
+            barrier, inc=1,
+            device_id={"expert": there // (n_x * n_c), "replica": there // n_c % n_x, "learner": there % n_c},
+            device_id_type=pl.DeviceIdType.MESH)
+
+    def block_of(half, zz):
+        return zz * n_c + (c if half else 1 - c)
+
+    for half in range(2):
+        for zz in range(n_z):
+            p = block_of(half, zz)
+            ids = route[p]
+            value = xs[p]
+            for k in range(top):
+                name = jnp.broadcast_to(ids[:, k:k + 1], (rows, d_loc))
+                for e in range(experts):
+                    xm[half, zz * slots + k * rows:zz * slots + (k + 1) * rows, e * d_loc:(e + 1) * d_loc] = (
+                        jnp.where(name == e, value.astype(f32), 0.0).astype(bf16))
+    pl.semaphore_wait(barrier, everyone - 1)
+
+    def sib_copy(n):
+        return remote(s_send.at[n], s_recv.at[n], s_ss.at[n], s_rs.at[n], sibling)
+
+    def z_copy(n, turn):
+        to = shift(z, turn, n_z)
+        return remote(z_send.at[n, to], z_recv.at[n, z], z_ss.at[n, to], z_rs.at[n, z], {"expert": to})
+
+    def z_arrival(n, turn):
+        source = shift(z, turn, n_z)
+        return remote(z_send.at[n, source], z_recv.at[n, source], z_ss.at[n, source], z_rs.at[n, source], {"expert": source})
+
+    def finish(n):
+        sib_copy(n).wait_recv()
+        both = own[lax.rem(n, 2)] + s_recv[n].astype(f32)
+        z_send[n] = both.astype(bf16).reshape(n_z, slots, 2 * LANE)
+        for turn in range(1, n_z):
+            z_copy(n, turn).start()
+
+    def step(n, carry):
+        s_send[n] = jnp.dot(xm[0], w1[n], preferred_element_type=f32).astype(bf16)
+        sib_copy(n).start()
+        own[lax.rem(n, 2)] = jnp.dot(xm[1], w1[n], preferred_element_type=f32)
+
+        @pl.when(n > 0)
+        def _():
+            finish(n - 1)
+        return carry
+
+    lax.fori_loop(0, chunks, step, 0)
+    finish(chunks - 1)
+
+    mine = route[me]
+
+    def h_copy(jj, xx):
+        owner = per_plane * x + jj
+        first = jj * f_loc // LANE
+        return remote(hid.at[pl.ds(first, span)], h_recv.at[me], h_ss.at[jj, xx], h_rs.at[me],
+                      {"expert": owner // n_c, "learner": owner % n_c, "replica": xx})
+
+    def is_me(jj, xx):
+        return (per_plane * x + jj == me) & (x == xx)
+
+    for n in range(chunks):
+        total = z_send[n, z].astype(f32)
+        for turn in range(1, n_z):
+            z_arrival(n, turn).wait_recv()
+        for turn in range(1, n_z):
+            total = total + z_recv[n, shift(z, turn, n_z)].astype(f32)
+        gate, up = total[:, :LANE], total[:, LANE:]
+        value = gate / (1.0 + jnp.exp(-gate)) * up
+        for k in range(top):
+            part = value[k * rows:(k + 1) * rows] * mine[:, top + k:top + k + 1]
+            hid[n, k * rows:(k + 1) * rows, :] = part.astype(bf16)
+        for jj in range(per_plane):
+            first = jj * f_loc // LANE
+            if first + span - 1 != n:
+                continue
+            for xx in range(n_x):
+                @pl.when(jnp.logical_not(is_me(jj, xx)))
+                def _(jj=jj, xx=xx):
+                    h_copy(jj, xx).start()
+
+                @pl.when(is_me(jj, xx))
+                def _(first=first):
+                    h_recv[me] = hid[first:first + span]
+
+    source_x = me // per_plane
+    for p in range(n_z * n_c):
+        @pl.when(jnp.logical_not((p == me) & (source_x == x)))
+        def _(p=p):
+            remote(hid.at[pl.ds(0, span)], h_recv.at[p], h_ss.at[0, 0], h_rs.at[p],
+                   {"expert": p // n_c, "learner": p % n_c, "replica": source_x}).wait_recv()
+
+    depth = span * LANE
+    for half in range(2):
+        for zz in range(n_z):
+            p = block_of(half, zz)
+            ids = route[p]
+            for e in range(experts):
+                for s in range(span):
+                    value = jnp.zeros((rows, LANE), f32)
+                    for k in range(top):
+                        name = jnp.broadcast_to(ids[:, k:k + 1], (rows, LANE))
+                        value = value + jnp.where(name == e, h_recv[p, s, k * rows:(k + 1) * rows, :].astype(f32), 0.0)
+                    wide[half, zz * rows:(zz + 1) * rows, e * depth + s * LANE:e * depth + (s + 1) * LANE] = value.astype(bf16)
+
+    def q_copy(n):
+        return remote(q_send.at[n], q_recv.at[n], q_ss.at[n], q_rs.at[n], sibling)
+
+    def o_copy(n, turn):
+        to = shift(z, turn, n_z)
+        return remote(o_send.at[n, to], o_recv.at[n, z], o_ss.at[n, to], o_rs.at[n, z], {"expert": to})
+
+    def o_arrival(n, turn):
+        source = shift(z, turn, n_z)
+        return remote(o_send.at[n, source], o_recv.at[n, source], o_ss.at[n, source], o_rs.at[n, source], {"expert": source})
+
+    def finish_out(n):
+        q_copy(n).wait_recv()
+        both = q_own[lax.rem(n, 2)] + q_recv[n].astype(f32)
+        o_send[n] = both.astype(bf16).reshape(n_z, rows, OUT_COLS)
+        for turn in range(1, n_z):
+            o_copy(n, turn).start()
+
+    out_chunks = w2.shape[1] // OUT_COLS
+
+    def step_out(n, carry):
+        columns = pl.ds(pl.multiple_of(n * OUT_COLS, OUT_COLS), OUT_COLS)
+        q_send[n] = jnp.dot(wide[0], w2[:, columns], preferred_element_type=f32).astype(bf16)
+        q_copy(n).start()
+        q_own[lax.rem(n, 2)] = jnp.dot(wide[1], w2[:, columns], preferred_element_type=f32)
+
+        @pl.when(n > 0)
+        def _():
+            finish_out(n - 1)
+        return carry
+
+    lax.fori_loop(0, out_chunks, step_out, 0)
+    finish_out(out_chunks - 1)
+
+    for n in range(out_chunks):
+        total = o_send[n, z].astype(f32)
+        for turn in range(1, n_z):
+            o_arrival(n, turn).wait_recv()
+        for turn in range(1, n_z):
+            total = total + o_recv[n, shift(z, turn, n_z)].astype(f32)
+        out[:, n * OUT_COLS:(n + 1) * OUT_COLS] = total.astype(bf16)
+
+    for n in range(chunks):
+        sib_copy(n).wait_send()
+        for turn in range(1, n_z):
+            z_copy(n, turn).wait_send()
+    for jj in range(per_plane):
+        for xx in range(n_x):
+            @pl.when(jnp.logical_not(is_me(jj, xx)))
+            def _(jj=jj, xx=xx):
+                h_copy(jj, xx).wait_send()
+    for n in range(out_chunks):
+        q_copy(n).wait_send()
+        for turn in range(1, n_z):
+            o_copy(n, turn).wait_send()
+
+
+def fused(sizes, xs, route, w1, w2):
+    n_z, n_x, top, experts, rows, d_loc, f_loc, span = sizes
+    n_dev = 2 * n_z
+    chunks, cols = w1.shape[0], w2.shape[1]
+    slots = top * rows
+    out_chunks = cols // OUT_COLS
+    bf16, f32 = jnp.bfloat16, jnp.float32
+    vmem, dma = pltpu.VMEM, pltpu.SemaphoreType.DMA
+    per_plane = n_dev // n_x
+    return pl.pallas_call(
+        functools.partial(kernel, sizes),
+        out_shape=jax.ShapeDtypeStruct((rows, cols), bf16),
+        in_specs=[pl.BlockSpec(memory_space=pltpu.VMEM)] * 4,
+        out_specs=pl.BlockSpec(memory_space=pltpu.VMEM),
+        scratch_shapes=[
+            vmem((2, n_z * slots, experts * d_loc), bf16),
+            vmem((chunks, n_z * slots, 2 * LANE), bf16),
+            vmem((chunks, n_z * slots, 2 * LANE), bf16),
+            vmem((2, n_z * slots, 2 * LANE), f32),
+            vmem((chunks, n_z, slots, 2 * LANE), bf16),
+            vmem((chunks, n_z, slots, 2 * LANE), bf16),
+            vmem((chunks, slots, LANE), bf16),
+            vmem((n_dev, span, slots, LANE), bf16),
+            vmem((2, n_z * rows, experts * span * LANE), bf16),
+            vmem((out_chunks, n_z * rows, OUT_COLS), bf16),
+            vmem((out_chunks, n_z * rows, OUT_COLS), bf16),
+            vmem((2, n_z * rows, OUT_COLS), f32),
+            vmem((out_chunks, n_z, rows, OUT_COLS), bf16),
+            vmem((out_chunks, n_z, rows, OUT_COLS), bf16),
+            dma((chunks,)), dma((chunks,)),
+            dma((chunks, n_z)), dma((chunks, n_z)),
+            dma((per_plane, n_x)), dma((n_dev,)),
+            dma((out_chunks,)), dma((out_chunks,)),
+            dma((out_chunks, n_z)), dma((out_chunks, n_z)),
+        ],
+        compiler_params=pltpu.CompilerParams(
+            collective_id=0, has_side_effects=True, vmem_limit_bytes=58 * 1024 * 1024),
+    )(xs, route, w1, w2)
+
+
+def kernel_sizes(n_z, n_c, n_x, top, experts, rows, d_loc, f_loc, units, cols):
+    if n_c != 2 or units % LANE or cols % OUT_COLS or rows % 16 or (n_z * n_c) % n_x:
+        return None
+    spans = [-(-((j + 1) * f_loc) // LANE) - j * f_loc // LANE for j in range(n_z * n_c // n_x)]
+    span = max(spans)
+    chunks = units // LANE
+    if any(j * f_loc // LANE + span > chunks for j in range(len(spans))):
+        return None
+    if 2 * n_z * top * rows * experts * d_loc * 2 > 8 * 1024 * 1024:
+        return None
+    return n_z, n_x, top, experts, rows, d_loc, f_loc, span
+
+
+def plain(tokens, route, w1, w2, n_x):
+    f32, bf16 = jnp.float32, jnp.bfloat16
+    n_z, n_c = lax.axis_size("expert"), lax.axis_size("learner")
+    c, x = lax.axis_index("learner"), lax.axis_index("replica")
+    n_dev = n_z * n_c
+    steps, rows_dev, _ = tokens.shape
+    experts, d_loc, _, units = w1.shape
+    f_loc, cols = w2.shape[1:]
+    top = route.shape[2] // 2
     piece = units // n_dev
-    f32, bf16 = jnp.float32, jnp.bfloat16
-
-    xs = lax.all_to_all(tokens, ROW_AXES, split_axis=2, concat_axis=1, tiled=True)
     n_rows = steps * rows_dev * n_dev
-    xs = xs.reshape(n_rows, d_loc)
-    share = gates / jnp.sum(gates, axis=2, keepdims=True)
-    route = jnp.concatenate([expert_ids.astype(f32), share], axis=2)
-    route = lax.all_gather(route, ROW_AXES, axis=1, tiled=True).reshape(n_rows, 2 * top)
+    xs = lax.all_to_all(tokens, ROW_AXES, split_axis=2, concat_axis=1, tiled=True).reshape(n_rows, d_loc)
+    route = route.reshape(n_dev, steps, rows_dev, 2 * top).swapaxes(0, 1).reshape(n_rows, 2 * top)
     ids = route[:, :top].T.astype(jnp.int32)
     share = route[:, top:].T
-
-    def take(scales, axis, first, count):
-        index = (first + jnp.arange(count)) // tile
-        onehot = (index[:, None] == jnp.arange(scales.shape[axis])[None, :]).astype(f32)
-        return jnp.moveaxis(
-            jnp.tensordot(scales, onehot, axes=([axis], [1]), precision=lax.Precision.HIGHEST), -1, axis
-        )
-
-    s1 = take(take(gate_up_scales, 1, me * d_loc, d_loc), 3, x * units, units)
-    w1 = (gate_up_tiles.astype(f32) * s1).astype(bf16).reshape(experts * d_loc, 2 * units)
-    s2 = take(take(down_scales, 1, me * f_loc, f_loc), 2, x * cols, cols)
-    w2 = (down_tiles.astype(f32) * s2).astype(bf16).reshape(experts * f_loc, cols)
-
+    w1 = w1.reshape(experts * d_loc, 2 * units)
+    w2 = w2.reshape(experts * f_loc, cols)
     names = jnp.arange(experts, dtype=jnp.int32)
     picked = ids[:, :, None] == names
     masked = jnp.where(picked[..., None], xs[None, :, None, :], jnp.zeros((), bf16))
@@ -86,6 +316,56 @@
     return jnp.sum(got.astype(f32), axis=0).astype(bf16)
 
 
+def body(tokens, gates, expert_ids, gate_up_tiles, gate_up_scales, down_tiles, down_scales):
+    steps, rows_dev, width = tokens.shape
+    top = expert_ids.shape[2]
+    n_z = lax.axis_size("expert")
+    n_c = lax.axis_size("learner")
+    n_x = lax.axis_size("replica")
+    n_dev = n_z * n_c
+    z, c, x = lax.axis_index("expert"), lax.axis_index("learner"), lax.axis_index("replica")
+    me = z * n_c + c
+    experts, d_loc, _, units = gate_up_tiles.shape
+    f_loc, cols = down_tiles.shape[1:]
+    tile = width // gate_up_scales.shape[1]
+    f32, bf16 = jnp.float32, jnp.bfloat16
+
+    def take(scales, axis, first, count):
+        index = (first + jnp.arange(count)) // tile
+        onehot = (index[:, None] == jnp.arange(scales.shape[axis])[None, :]).astype(f32)
+        return jnp.moveaxis(
+            jnp.tensordot(scales, onehot, axes=([axis], [1]), precision=lax.Precision.HIGHEST), -1, axis
+        )
+
+    s1 = take(take(gate_up_scales, 1, me * d_loc, d_loc), 3, x * units, units)
+    w1 = (gate_up_tiles.astype(f32) * s1).astype(bf16)
+    s2 = take(take(down_scales, 1, me * f_loc, f_loc), 2, x * cols, cols)
+    w2 = (down_tiles.astype(f32) * s2).astype(bf16)
+
+
+    rows = steps * rows_dev
+    share = gates / jnp.sum(gates, axis=2, keepdims=True)
+    route = jnp.concatenate([expert_ids.astype(f32), share], axis=2).reshape(1, rows, 2 * top)
+    route = lax.all_gather(route, ROW_AXES, axis=0, tiled=True)
+    sizes = kernel_sizes(n_z, n_c, n_x, top, experts, rows, d_loc, f_loc, units, cols)
+    if sizes is None:
+        return plain(tokens, route, w1, w2, n_x)
+    xs = jnp.swapaxes(tokens.reshape(rows, n_dev, d_loc), 0, 1)
+    xs = lax.all_to_all(xs, ROW_AXES, split_axis=0, concat_axis=0, tiled=True)
+    route = jnp.pad(route, ((0, 0), (0, 0), (0, LANE - 2 * top)))
+    w1 = w1.reshape(experts * d_loc, 2, units // LANE, LANE)
+    w1 = w1.transpose(2, 0, 1, 3).reshape(units // LANE, experts * d_loc, 2 * LANE)
+    depth = sizes[-1] * LANE
+    offset = lax.rem(lax.rem(me, n_dev // n_x) * f_loc, LANE)
+    options = sorted({j * f_loc % LANE for j in range(n_dev // n_x)})
+    padded = 0
+    for option in options:
+        case = jnp.pad(w2, ((0, 0), (option, depth - f_loc - option), (0, 0)))
+        padded = padded + jnp.where(offset == option, case, jnp.zeros((), bf16))
+    out = fused(sizes, xs, route, w1, padded.reshape(experts * depth, cols))
+    return out.reshape(steps, rows_dev, cols)
+
+
 def solution(mesh):
     placed = (
         P(None, ("group", "expert", "learner"), None),

time: 198 us -> 189 us (0.955)
  Pallas kernels: 0 us -> 93.7 us
  waiting for transfers between devices: 45.7 us -> 0.01 us
  blocking collectives: 50.9 us -> 13.3 us
  matrix products: 25.9 us -> 15.6 us
  starting transfers between devices: 15.6 us -> 6.33 us
  local copies, waits for them, and re-layouts: 48.4 us -> 54.4 us
  other arithmetic: 10 us -> 4.19 us
    pallas_call x0 -> x1, Pallas kernels: none -> 93.7 us  [fused(): pl.pallas_call(functools.partial(kernel, sizes), out_shape=jax.ShapeDtype...]
    all_to_all x1 -> x0, blocking collectives: 36 us -> none  [body(): lax.all_to_all(half, 'expert', split_axis=0, concat_axis=0, tiled=True)]
    all_to_all x2 -> x1, waiting for transfers between devices: 31.5 us -> 0.01 us  [body(): xs = lax.all_to_all(xs, ROW_AXES, split_axis=0, concat_axis=0, tiled=True)]
    reshape x0 -> x4, local copies, waits for them, and re-layouts: none -> 23 us  [the longest x1 11.1 us: body(): w1 = w1.reshape(experts * d_loc, 2, units // LANE, LANE)]
    unnamed x22 -> x6, local copies, waits for them, and re-layouts: 22 us -> 2.9 us
    transpose x1, local copies, waits for them, and re-layouts: 1.28 us -> 16.2 us  [body(): w1.transpose(2, 0, 1, 3).reshape(units // LANE, experts * d_loc, 2 * LANE)]
    ppermute x4 -> x0, waiting for transfers between devices: 14.2 us -> none  [the longest x2 8.48 us: body(): pieces.append(lax.ppermute(hidden, ('expert', 'replica', 'learner'), pairs))]
    dot_general x2 -> x0, matrix products: 9.95 us -> none  [the longest x1 8.08 us: body(): jnp.dot(masked.reshape(top * n_rows, experts * d_loc), w1, preferred_elem...]
  transfers between devices with their start and end apart: 6 -> 1, of which waited for: 4 -> 0; matrix products, arithmetic and copies ran while one was open for 16% -> 37% of each run, Pallas kernels for 0% -> 0%
where the time goes in v2:
time: 189 us; the launch traced here: 188 us
  Pallas kernels  93.7 us (50%)
  local copies, waits for them, and re-layouts  54.4 us (29%)
  matrix products  15.6 us (8%)
  blocking collectives  13.3 us (7%)
  starting transfers between devices  6.33 us (3%)
  other arithmetic  4.19 us (2%)
    pallas_call x1, Pallas kernels, fused(): pl.pallas_call(functools.partial(kernel, sizes), out_shape=jax.ShapeDtype...  93.7 us
    transpose x1, local copies, waits for them, and re-layouts, body(): w1.transpose(2, 0, 1, 3).reshape(units // LANE, experts * d_loc, 2 * LANE)  16.2 us
    dot_general x4, matrix products, take(): jnp.tensordot(scales, onehot, axes=([axis], [1]), precision=lax.Precision...  15.6 us
    all_gather x1, blocking collectives, body(): route = lax.all_gather(route, ROW_AXES, axis=0, tiled=True)  13.3 us
    convert_element_type x1, local copies, waits for them, and re-layouts, body(): w1 = (gate_up_tiles.astype(f32) * s1).astype(bf16)  11.4 us
    reshape x1, local copies, waits for them, and re-layouts, body(): w1 = w1.reshape(experts * d_loc, 2, units // LANE, LANE)  11.1 us
    reshape x1, local copies, waits for them, and re-layouts, body(): w1.transpose(2, 0, 1, 3).reshape(units // LANE, experts * d_loc, 2 * LANE)  10.9 us
    all_to_all x1, starting transfers between devices, body(): xs = lax.all_to_all(xs, ROW_AXES, split_axis=0, concat_axis=0, tiled=True)  6.33 us
  transfers between devices with their start and end apart: 1, of which 0 were waited for; matrix products, arithmetic and copies ran while one was open for 37% of the time, Pallas kernels for 0%

profile of v2, /device:TPU:0, one launch (start us, length us, event | category | flops | bytes accessed | tf_op | source)
XLA Modules:
  0.0 187.6 jit_solution(10566060107469199522)
XLA Ops:
  0.0 0.0 copy-start
  0.0 1.2 copy.25
  1.2 1.0 copy.32
  2.2 6.3 %all-to-all-start = ((bf16[8,64,512]{2,1,0:T(8,128)(2,1)}), bf16[8,64,512]{2,1,0:T(8,128)(2,1)}, u32[]{:S(2)}, u32[]{:S(2)}) async-start(bf16[8,64,512]{2,1,0:T(8,128)(2,1)} %bitcast.36), calls=%async_computation | async-start | bytes 1048576 | tf_op jit(solution)/shard_map/all_to_all | solution.py:354
  8.5 0.8 fusion.23
  9.3 0.7 convert_element_type.25
  10.0 0.0 copy-done
  10.1 0.3 convolution_bitcast_fusion
  10.3 1.6 convolution_bitcast_fusion.1
  12.0 9.8 %multiply_convert_fusion = bf16[4,512,2,768]{3,1,2,0:T(8,128)(2,1)} fusion(bf16[4,512,2,768]{3,2,1,0:T(2,128)(2,1)} %param.10, f32[4,512,2,12]{1,3,2,0:T(8,128)S(1)} %convolution_bitcast_fusion, s32[768]{0:T(1024)S(1)} %add_select_fusion.1), kind=kOutput, calls=%fused_computation | convolution fusion | flops 462431232 | bytes 12782592 | tf_op jit(solution)/shard_map/dot_general | solution.py:337
  21.8 0.1 reshape.96
  21.9 13.3 %all_gather.3 = f32[8,64,4]{1,2,0:T(4,128)S(1)} all-gather(f32[1,64,4]{1,2,0:T(4,128)S(1)} %reshape.96), channel_id=1, replica_groups=mesh['group'=2,'expert'=4,'replica'=2,'learner'=2] {'expert','learner'}, dimensions={0}, use_global_device_ids=true | all-gather | bytes 9216 | tf_op jit(solution)/shard_map/all_gather | solution.py:349
  35.1 0.1 copy.17
  35.3 11.4 %copy.20 = bf16[4,512,2,768]{1,0,3,2:T(4,128)(2,1)} copy(bf16[4,512,2,768]{3,1,2,0:T(8,128)(2,1)} %multiply_convert_fusion) | data formatting | bytes 12582912 | tf_op jit(solution)/shard_map/convert_element_type | solution.py:341
  46.7 11.1 %reshape.97 = bf16[2048,2,6,128]{0,3,2,1:T(8,128)(2,1)} reshape(bf16[4,512,2,768]{1,0,3,2:T(4,128)(2,1)} %copy.20) | data formatting | bytes 12582912 | tf_op jit(solution)/shard_map/reshape | solution.py:356
  57.7 16.2 %copy.21 = bf16[6,2048,2,128]{3,2,1,0:T(2,128)(2,1)} copy(bf16[6,2048,2,128]{1,3,0,2:T(8,128)(2,1)} %bitcast.37) | data formatting | bytes 12582912 | tf_op jit(solution)/shard_map/transpose | solution.py:357
  73.9 0.0 copy-start.1
  73.9 10.9 %reshape.98.w1 = bf16[6,2048,256]{2,1,0:T(8,128)(2,1)} reshape(bf16[6,2048,2,128]{3,2,1,0:T(2,128)(2,1)} %copy.21) | data formatting | bytes 12582912 | tf_op jit(solution)/shard_map/reshape | solution.py:357
  84.8 0.7 pad.12.route
  85.6 0.0 copy-done.1
  85.6 4.0 %multiply_convert_fusion.1 = bf16[4,192,2048]{2,1,0:T(8,128)(2,1)S(1)} fusion(bf16[4,192,2048]{2,1,0:T(8,128)(2,1)S(1)} %copy-done.1, f32[4,192,32]{1,2,0:T(8,128)} %convolution_bitcast_fusion.1, s32[2048]{0:T(1024)S(1)} %add_select_fusion), kind=kOutput, calls=%fused_computation.1 | convolution fusion | flops 608763904 | bytes 6397952 | tf_op jit(solution)/shard_map/dot_general | solution.py:337
  89.5 2.7 %select_add_fusion = bf16[4,256,2048]{2,1,0:T(8,128)(2,1)} fusion(bf16[4,192,2048]{2,1,0:T(8,128)(2,1)S(1)} %multiply_convert_fusion.1, pred[]{:T(512)S(6)} %eq.71, pred[]{:T(512)S(6)} %eq.64), kind=kLoop, calls=%fused_computation.2 | loop fusion | flops 12582912 | bytes 7340034 | tf_op jit(solution)/shard_map/add | solution.py:364
  92.2 0.0 all-to-all-done.xs
  92.2 93.7 %shard_map.73 = bf16[64,2048]{1,0:T(8,128)(2,1)} custom-call(bf16[8,64,512]{2,1,0:T(8,128)(2,1)} %all-to-all-done.xs, f32[8,64,128]{2,1,0:T(8,128)} %pad.12.route, bf16[6,2048,256]{2,1,0:T(8,128)(2,1)} %reshape.98.w1, bf16[1024,2048]{1,0:T(8,128)(2,1)} %bitcast.38), custom_call_target="tpu_custom_call" | custom-call | tf_op jit(solution)/shard_map/pallas_call | solution.py:214
  186.0 1.7 copy.34
  (6 shorter events, 0.1 us)
Async XLA Ops:
  0.0 10.0 %copy-start = (f32[4,32,2,12]{1,2,3,0:T(2,128)S(1)}, f32[4,32,2,12]{1,2,3,0:T(2,128)}, u32[]{:S(2)}) copy-start(f32[4,32,2,12]{1,2,3,0:T(2,128)} %param.11) | copy-start | bytes 36868
  2.2 90.0 %all-to-all-start = ((bf16[8,64,512]{2,1,0:T(8,128)(2,1)}), bf16[8,64,512]{2,1,0:T(8,128)(2,1)}, u32[]{:S(2)}, u32[]{:S(2)}) async-start(bf16[8,64,512]{2,1,0:T(8,128)(2,1)} %bitcast.36), calls=%async_computation | async-start | bytes 1048576 | tf_op jit(solution)/shard_map/all_to_all | solution.py:354
  73.9 11.7 %copy-start.1 = (bf16[4,192,2048]{2,1,0:T(8,128)(2,1)S(1)}, bf16[4,192,2048]{2,1,0:T(8,128)(2,1)}, u32[]{:S(2)}) copy-start(bf16[4,192,2048]{2,1,0:T(8,128)(2,1)} %param.12) | copy-start | bytes 9437188

commit v3 on v2

--- a/solution.py
+++ b/solution.py
@@ -16,9 +16,9 @@
     return lax.rem(index + by, count)
 
 
-def kernel(sizes, xs, route, w1, w2, out, xm, s_send, s_recv, own, z_send, z_recv, hid, h_recv,
+def kernel(sizes, xs, my_route, w1_in, w2_in, out, route, w1, w2, xm, s_send, s_recv, own, z_send, z_recv, hid, h_recv,
            wide, q_send, q_recv, q_own, o_send, o_recv,
-           s_ss, s_rs, z_ss, z_rs, h_ss, h_rs, q_ss, q_rs, o_ss, o_rs):
+           w1_s, w2_s, r_ss, r_rs, s_ss, s_rs, z_ss, z_rs, h_ss, h_rs, q_ss, q_rs, o_ss, o_rs):
     n_z, n_x, top, experts, rows, d_loc, f_loc, span = sizes
     n_c = 2
     f32, bf16 = jnp.float32, jnp.bfloat16
@@ -34,6 +34,26 @@
             src_ref=src, dst_ref=dst, send_sem=send, recv_sem=recv,
             device_id=device, device_id_type=pl.DeviceIdType.MESH)
 
+    depth = span * LANE
+
+    def w1_copy(n, e, g):
+        return pltpu.make_async_copy(
+            w1_in.at[e, g, :, pl.ds(pl.multiple_of(n * LANE, LANE), LANE)],
+            w1.at[n, pl.ds(e * d_loc, d_loc), pl.ds(g * LANE, LANE)], w1_s.at[n, e, g])
+
+    offset = lax.rem(lax.rem(me, per_plane) * f_loc, LANE)
+
+    def w2_copy(e):
+        return pltpu.make_async_copy(
+            w2_in.at[e], w2.at[pl.ds(pl.multiple_of(e * depth + offset, 16), f_loc)], w2_s.at[e])
+
+    for n in range(chunks):
+        for e in range(experts):
+            for g in range(2):
+                w1_copy(n, e, g).start()
+    for e in range(experts):
+        w2_copy(e).start()
+
     barrier = pltpu.get_barrier_semaphore()
     everyone = n_z * n_c * n_x
     here = (z * n_x + x) * n_c + c
@@ -46,6 +66,35 @@
 
     def block_of(half, zz):
         return zz * n_c + (c if half else 1 - c)
+
+    pl.semaphore_wait(barrier, everyone - 1)
+    blocks = n_z * n_c
+
+    def route_copy(turn):
+        to = shift(me, turn, blocks)
+        return remote(my_route, route.at[me], r_ss.at[to], r_rs.at[me],
+                      {"expert": to // n_c, "learner": to % n_c})
+
+    def route_arrival(turn):
+        source = shift(me, turn, blocks)
+        return remote(my_route, route.at[source], r_ss.at[source], r_rs.at[source],
+                      {"expert": source // n_c, "learner": source % n_c})
+
+    for turn in range(1, blocks):
+        route_copy(turn).start()
+    route[me] = my_route[...]
+    if depth > f_loc:
+        gap = depth - f_loc
+        for option in sorted({j * f_loc % LANE for j in range(per_plane)}):
+            @pl.when(offset == option)
+            def _(option=option):
+                for e in range(experts):
+                    if option:
+                        w2[e * depth:e * depth + option] = jnp.zeros((option, w2.shape[1]), bf16)
+                    if gap > option:
+                        w2[e * depth + option + f_loc:(e + 1) * depth] = jnp.zeros((gap - option, w2.shape[1]), bf16)
+    for turn in range(1, blocks):
+        route_arrival(turn).wait_recv()
 
     for half in range(2):
         for zz in range(n_z):
@@ -57,7 +106,6 @@
                 for e in range(experts):
                     xm[half, zz * slots + k * rows:zz * slots + (k + 1) * rows, e * d_loc:(e + 1) * d_loc] = (
                         jnp.where(name == e, value.astype(f32), 0.0).astype(bf16))
-    pl.semaphore_wait(barrier, everyone - 1)
 
     def sib_copy(n):
         return remote(s_send.at[n], s_recv.at[n], s_ss.at[n], s_rs.at[n], sibling)
@@ -78,6 +126,9 @@
             z_copy(n, turn).start()
 
     def step(n, carry):
+        for e in range(experts):
+            for g in range(2):
+                w1_copy(n, e, g).wait()
         s_send[n] = jnp.dot(xm[0], w1[n], preferred_element_type=f32).astype(bf16)
         sib_copy(n).start()
         own[lax.rem(n, 2)] = jnp.dot(xm[1], w1[n], preferred_element_type=f32)
@@ -132,7 +183,6 @@
             remote(hid.at[pl.ds(0, span)], h_recv.at[p], h_ss.at[0, 0], h_rs.at[p],
                    {"expert": p // n_c, "learner": p % n_c, "replica": source_x}).wait_recv()
 
-    depth = span * LANE
     for half in range(2):
         for zz in range(n_z):
             p = block_of(half, zz)
@@ -164,6 +214,8 @@
             o_copy(n, turn).start()
 
     out_chunks = w2.shape[1] // OUT_COLS
+    for e in range(experts):
+        w2_copy(e).wait()
 
     def step_out(n, carry):
         columns = pl.ds(pl.multiple_of(n * OUT_COLS, OUT_COLS), OUT_COLS)
@@ -187,6 +239,8 @@
             total = total + o_recv[n, shift(z, turn, n_z)].astype(f32)
         out[:, n * OUT_COLS:(n + 1) * OUT_COLS] = total.astype(bf16)
 
+    for turn in range(1, blocks):
+        route_copy(turn).wait_send()
     for n in range(chunks):
         sib_copy(n).wait_send()
         for turn in range(1, n_z):
@@ -205,7 +259,7 @@
 def fused(sizes, xs, route, w1, w2):
     n_z, n_x, top, experts, rows, d_loc, f_loc, span = sizes
     n_dev = 2 * n_z
-    chunks, cols = w1.shape[0], w2.shape[1]
+    chunks, cols = w1.shape[3] // LANE, w2.shape[2]
     slots = top * rows
     out_chunks = cols // OUT_COLS
     bf16, f32 = jnp.bfloat16, jnp.float32
@@ -214,9 +268,12 @@
     return pl.pallas_call(
         functools.partial(kernel, sizes),
         out_shape=jax.ShapeDtypeStruct((rows, cols), bf16),
-        in_specs=[pl.BlockSpec(memory_space=pltpu.VMEM)] * 4,
+        in_specs=[pl.BlockSpec(memory_space=pltpu.VMEM)] * 2 + [pl.BlockSpec(memory_space=pl.ANY)] * 2,
         out_specs=pl.BlockSpec(memory_space=pltpu.VMEM),
         scratch_shapes=[
+            vmem((n_dev, rows, LANE), f32),
+            vmem((chunks, experts * d_loc, 2 * LANE), bf16),
+            vmem((experts * span * LANE, cols), bf16),
             vmem((2, n_z * slots, experts * d_loc), bf16),
             vmem((chunks, n_z * slots, 2 * LANE), bf16),
             vmem((chunks, n_z * slots, 2 * LANE), bf16),
@@ -231,6 +288,8 @@
             vmem((2, n_z * rows, OUT_COLS), f32),
             vmem((out_chunks, n_z, rows, OUT_COLS), bf16),
             vmem((out_chunks, n_z, rows, OUT_COLS), bf16),
+            dma((chunks, experts, 2)), dma((experts,)),
+            dma((n_dev,)), dma((n_dev,)),
             dma((chunks,)), dma((chunks,)),
             dma((chunks, n_z)), dma((chunks, n_z)),
             dma((per_plane, n_x)), dma((n_dev,)),
@@ -346,23 +405,14 @@
     rows = steps * rows_dev
     share = gates / jnp.sum(gates, axis=2, keepdims=True)
     route = jnp.concatenate([expert_ids.astype(f32), share], axis=2).reshape(1, rows, 2 * top)
-    route = lax.all_gather(route, ROW_AXES, axis=0, tiled=True)
     sizes = kernel_sizes(n_z, n_c, n_x, top, experts, rows, d_loc, f_loc, units, cols)
     if sizes is None:
+        route = lax.all_gather(route, ROW_AXES, axis=0, tiled=True)
         return plain(tokens, route, w1, w2, n_x)
     xs = jnp.swapaxes(tokens.reshape(rows, n_dev, d_loc), 0, 1)
     xs = lax.all_to_all(xs, ROW_AXES, split_axis=0, concat_axis=0, tiled=True)
-    route = jnp.pad(route, ((0, 0), (0, 0), (0, LANE - 2 * top)))
-    w1 = w1.reshape(experts * d_loc, 2, units // LANE, LANE)
-    w1 = w1.transpose(2, 0, 1, 3).reshape(units // LANE, experts * d_loc, 2 * LANE)
-    depth = sizes[-1] * LANE
-    offset = lax.rem(lax.rem(me, n_dev // n_x) * f_loc, LANE)
-    options = sorted({j * f_loc % LANE for j in range(n_dev // n_x)})
-    padded = 0
-    for option in options:
-        case = jnp.pad(w2, ((0, 0), (option, depth - f_loc - option), (0, 0)))
-        padded = padded + jnp.where(offset == option, case, jnp.zeros((), bf16))
-    out = fused(sizes, xs, route, w1, padded.reshape(experts * depth, cols))
+    route = jnp.pad(route[0], ((0, 0), (0, LANE - 2 * top)))
+    out = fused(sizes, xs, route, jnp.swapaxes(w1, 1, 2), w2)
     return out.reshape(steps, rows_dev, cols)
 
 

time: 189 us -> 128 us (0.68)
  local copies, waits for them, and re-layouts: 54.4 us -> 5.37 us
  blocking collectives: 13.3 us -> 0 us
  Pallas kernels: 93.7 us -> 99.5 us
  other arithmetic: 4.19 us -> 1.52 us
    reshape x3 -> x0, local copies, waits for them, and re-layouts: 22.1 us -> none  [the longest x1 11.1 us: body(): w1 = w1.reshape(experts * d_loc, 2, units // LANE, LANE)]
    transpose x1 -> x0, local copies, waits for them, and re-layouts: 16.2 us -> none  [body(): w1.transpose(2, 0, 1, 3).reshape(units // LANE, experts * d_loc, 2 * LANE)]
    all_gather x1 -> x0, blocking collectives: 13.3 us -> none  [body(): route = lax.all_gather(route, ROW_AXES, axis=0, tiled=True)]
    convert_element_type x1 -> x0, local copies, waits for them, and re-layouts: 11.4 us -> none  [body(): w1 = (gate_up_tiles.astype(f32) * s1).astype(bf16)]
    pallas_call x1, Pallas kernels: 93.7 us -> 99.5 us  [fused(): pl.pallas_call(functools.partial(kernel, sizes), out_shape=jax.ShapeDtype...]
    add x1 -> x0, other arithmetic: 2.67 us -> none  [body(): padded = padded + jnp.where(offset == option, case, jnp.zeros((), bf16))]
  transfers between devices with their start and end apart: 1 -> 1, of which waited for: 0 -> 0; matrix products, arithmetic and copies ran while one was open for 37% -> 13% of each run, Pallas kernels for 0% -> 0%
where the time goes in v3:
time: 128 us
  Pallas kernels  99.5 us (78%)
  matrix products  15 us (12%)
  starting transfers between devices  6.33 us (5%)
  local copies, waits for them, and re-layouts  5.37 us (4%)
  other arithmetic  1.52 us (1%)
    pallas_call x1, Pallas kernels, fused(): pl.pallas_call(functools.partial(kernel, sizes), out_shape=jax.ShapeDtype...  99.5 us
    dot_general x4, matrix products, take(): jnp.tensordot(scales, onehot, axes=([axis], [1]), precision=lax.Precision...  15 us
    all_to_all x1, starting transfers between devices, body(): xs = lax.all_to_all(xs, ROW_AXES, split_axis=0, concat_axis=0, tiled=True)  6.33 us
    unnamed x8, local copies, waits for them, and re-layouts  3.7 us
  transfers between devices with their start and end apart: 1, of which 0 were waited for; matrix products, arithmetic and copies ran while one was open for 13% of the time, Pallas kernels for 0%

profile of v3, /device:TPU:0, one launch (start us, length us, event | category | flops | bytes accessed | tf_op | source)
XLA Modules:
  0.0 127.8 jit_solution(13785619356668692267)
XLA Ops:
  0.0 0.0 copy-start
  0.0 1.2 copy.17
  1.2 1.0 copy.24
  2.2 6.3 %all-to-all-start = ((bf16[8,64,512]{2,1,0:T(8,128)(2,1)}), bf16[8,64,512]{2,1,0:T(8,128)(2,1)S(1)}, u32[]{:S(2)}, u32[]{:S(2)}) async-start(bf16[8,64,512]{2,1,0:T(8,128)(2,1)} %bitcast.33), calls=%async_computation | async-start | bytes 1048576 | tf_op jit(solution)/shard_map/all_to_all | solution.py:413
  8.5 0.8 fusion.24
  9.3 0.7 convert_element_type.21
  10.0 0.1 copy.11
  10.1 0.0 copy-start.1
  10.2 0.6 pad.4.my_route
  10.8 0.0 copy-done
  10.8 0.4 convolution_bitcast_fusion
  11.2 1.5 %convolution_bitcast_fusion.1 = f32[4,192,32]{1,2,0:T(8,128)S(1)} fusion(s32[192]{0:T(256)S(1)} %and_select_fusion, f32[4,12,32]{2,0,1:T(4,128)} %param.13), kind=kOutput, calls=%fused_computation.4 | convolution fusion | flops 3541248 | bytes 105216 | tf_op jit(solution)/shard_map/dot_general | solution.py:396
  12.7 5.7 %multiply_convert_fusion.1.w2_in = bf16[4,192,2048]{2,1,0:T(8,128)(2,1)} fusion(bf16[4,192,2048]{2,1,0:T(8,128)(2,1)} %param.12, f32[4,192,32]{1,2,0:T(8,128)S(1)} %convolution_bitcast_fusion.1, s32[2048]{0:T(1024)S(1)} %add_select_fusion), kind=kOutput, calls=%fused_computation.2 | convolution fusion | flops 608763904 | bytes 6397952 | tf_op jit(solution)/shard_map/dot_general | solution.py:396
  18.4 0.0 copy-done.1
  18.4 7.4 %fusion.w1_in = bf16[4,2,512,768]{3,2,1,0:T(8,128)(2,1)} fusion(bf16[4,512,2,768]{3,2,1,0:T(2,128)(2,1)S(1)} %copy-done.1, f32[4,512,2,12]{1,3,2,0:T(8,128)S(1)} %convolution_bitcast_fusion, s32[768]{0:T(1024)S(1)} %add_select_fusion.1), kind=kOutput, calls=%fused_computation.1 | convolution fusion | flops 462431232 | bytes 12782592 | tf_op jit(solution)/shard_map/dot_general | solution.py:396
  25.8 0.0 all-to-all-done.xs
  25.8 0.0 copy-start.2
  25.8 0.8 copy-done.2
  26.6 99.5 %shard_map.73 = bf16[64,2048]{1,0:T(8,128)(2,1)} custom-call(bf16[8,64,512]{2,1,0:T(8,128)(2,1)} %copy-done.2, f32[64,128]{1,0:T(8,128)} %pad.4.my_route, bf16[4,2,512,768]{3,2,1,0:T(8,128)(2,1)} %fusion.w1_in, bf16[4,192,2048]{2,1,0:T(8,128)(2,1)} %multiply_convert_fusion.1.w2_in), custom_call_target="tpu_custom_call" | custom-call | tf_op jit(solution)/shard_map/pallas_call | solution.py:268
  126.1 1.7 %copy.26 = bf16[4,16,2048]{2,1,0:T(8,128)(2,1)} copy(bf16[4,16,2048]{2,1,0:T(8,128)(2,1)} %bitcast.35) | data formatting | bytes 524288
  (5 shorter events, 0.1 us)
Async XLA Ops:
  0.0 10.8 %copy-start = (f32[4,32,2,12]{1,2,3,0:T(2,128)S(1)}, f32[4,32,2,12]{1,2,3,0:T(2,128)}, u32[]{:S(2)}) copy-start(f32[4,32,2,12]{1,2,3,0:T(2,128)} %param.11) | copy-start | bytes 36868
  2.2 23.6 %all-to-all-start = ((bf16[8,64,512]{2,1,0:T(8,128)(2,1)}), bf16[8,64,512]{2,1,0:T(8,128)(2,1)S(1)}, u32[]{:S(2)}, u32[]{:S(2)}) async-start(bf16[8,64,512]{2,1,0:T(8,128)(2,1)} %bitcast.33), calls=%async_computation | async-start | bytes 1048576 | tf_op jit(solution)/shard_map/all_to_all | solution.py:413
  10.1 8.3 %copy-start.1 = (bf16[4,512,2,768]{3,2,1,0:T(2,128)(2,1)S(1)}, bf16[4,512,2,768]{3,2,1,0:T(2,128)(2,1)}, u32[]{:S(2)}) copy-start(bf16[4,512,2,768]{3,2,1,0:T(2,128)(2,1)} %param.10) | copy-start | bytes 18874372
  25.8 0.8 copy-start.2

commit v4 on v3

--- a/solution.py
+++ b/solution.py
@@ -16,9 +16,9 @@
     return lax.rem(index + by, count)
 
 
-def kernel(sizes, xs, my_route, w1_in, w2_in, out, route, w1, w2, xm, s_send, s_recv, own, z_send, z_recv, hid, h_recv,
-           wide, q_send, q_recv, q_own, o_send, o_recv,
-           w1_s, w2_s, r_ss, r_rs, s_ss, s_rs, z_ss, z_rs, h_ss, h_rs, q_ss, q_rs, o_ss, o_rs):
+def kernel(sizes, xs, my_route, w1_in, w2_in, out, route, w1, w2, xm, s_send, s_recv, own, z_send, z_recv, z_pass, hid, h_recv,
+           wide, q_send, q_recv, q_own, o_send, o_recv, o_pass,
+           w1_s, w2_s, r_ss, r_rs, s_ss, s_rs, z_ss, z_rs, z_ps, h_ss, h_rs, q_ss, q_rs, o_ss, o_rs, o_ps):
     n_z, n_x, top, experts, rows, d_loc, f_loc, span = sizes
     n_c = 2
     f32, bf16 = jnp.float32, jnp.bfloat16
@@ -107,23 +107,55 @@
                     xm[half, zz * slots + k * rows:zz * slots + (k + 1) * rows, e * d_loc:(e + 1) * d_loc] = (
                         jnp.where(name == e, value.astype(f32), 0.0).astype(bf16))
 
+    near = z + 1 - 2 * lax.rem(z, 2)
+    far_mid = jnp.where(z < 2, 2, 1)
+    far_end = jnp.where(z < 2, 3, 0)
+    at_end = (z == 0) | (z == n_z - 1)
+
+    def line(send, recv, relay, own, ss, rs, ps):
+        def direct(n, block, slot):
+            return remote(send.at[n, block], recv.at[n, slot], ss.at[n, block], rs.at[n, slot], {"expert": block})
+
+        def hand(n, block, slot):
+            return remote(send.at[n, block], relay.at[n, slot], ss.at[n, block], ps.at[n, slot], {"expert": near})
+
+        def begin(n):
+            @pl.when(at_end)
+            def _():
+                for slot, block in ((1, far_end), (0, far_mid)):
+                    send[n, block] = own[n, block].astype(bf16)
+                    hand(n, block, slot).start()
+            send[n, near] = own[n, near].astype(bf16)
+            direct(n, near, 0).start()
+
+        def pass_on(n):
+            @pl.when(jnp.logical_not(at_end))
+            def _():
+                for slot, block in ((1, far_end), (0, far_mid)):
+                    hand(n, block, slot).wait_recv()
+                    send[n, block] = (own[n, block] + relay[n, slot].astype(f32)).astype(bf16)
+                    direct(n, block, 1).start()
+
+        def total(n):
+            direct(n, near, 0).wait_recv()
+            direct(n, far_mid, 1).wait_recv()
+            return own[n, z] + recv[n, 0].astype(f32) + recv[n, 1].astype(f32)
+
+        def close(n):
+            for block in (near, far_mid, far_end):
+                direct(n, block, 0).wait_send()
+
+        return begin, pass_on, total, close
+
     def sib_copy(n):
         return remote(s_send.at[n], s_recv.at[n], s_ss.at[n], s_rs.at[n], sibling)
 
-    def z_copy(n, turn):
-        to = shift(z, turn, n_z)
-        return remote(z_send.at[n, to], z_recv.at[n, z], z_ss.at[n, to], z_rs.at[n, z], {"expert": to})
-
-    def z_arrival(n, turn):
-        source = shift(z, turn, n_z)
-        return remote(z_send.at[n, source], z_recv.at[n, source], z_ss.at[n, source], z_rs.at[n, source], {"expert": source})
+    begin, pass_on, total_of, close = line(z_send, z_recv, z_pass, own, z_ss, z_rs, z_ps)
 
     def finish(n):
         sib_copy(n).wait_recv()
-        both = own[lax.rem(n, 2)] + s_recv[n].astype(f32)
-        z_send[n] = both.astype(bf16).reshape(n_z, slots, 2 * LANE)
-        for turn in range(1, n_z):
-            z_copy(n, turn).start()
+        own[n] += s_recv[n].astype(f32).reshape(n_z, slots, 2 * LANE)
+        begin(n)
 
     def step(n, carry):
         for e in range(experts):
@@ -131,15 +163,21 @@
                 w1_copy(n, e, g).wait()
         s_send[n] = jnp.dot(xm[0], w1[n], preferred_element_type=f32).astype(bf16)
         sib_copy(n).start()
-        own[lax.rem(n, 2)] = jnp.dot(xm[1], w1[n], preferred_element_type=f32)
+        own[n] = jnp.dot(xm[1], w1[n], preferred_element_type=f32).reshape(n_z, slots, 2 * LANE)
 
         @pl.when(n > 0)
         def _():
             finish(n - 1)
+
+        @pl.when(n > 1)
+        def _():
+            pass_on(n - 2)
         return carry
 
     lax.fori_loop(0, chunks, step, 0)
     finish(chunks - 1)
+    for n in range(max(chunks - 2, 0), chunks):
+        pass_on(n)
 
     mine = route[me]
 
@@ -153,11 +191,7 @@
         return (per_plane * x + jj == me) & (x == xx)
 
     for n in range(chunks):
-        total = z_send[n, z].astype(f32)
-        for turn in range(1, n_z):
-            z_arrival(n, turn).wait_recv()
-        for turn in range(1, n_z):
-            total = total + z_recv[n, shift(z, turn, n_z)].astype(f32)
+        total = total_of(n)
         gate, up = total[:, :LANE], total[:, LANE:]
         value = gate / (1.0 + jnp.exp(-gate)) * up
         for k in range(top):
@@ -198,20 +232,12 @@
     def q_copy(n):
         return remote(q_send.at[n], q_recv.at[n], q_ss.at[n], q_rs.at[n], sibling)
 
-    def o_copy(n, turn):
-        to = shift(z, turn, n_z)
-        return remote(o_send.at[n, to], o_recv.at[n, z], o_ss.at[n, to], o_rs.at[n, z], {"expert": to})
-
-    def o_arrival(n, turn):
-        source = shift(z, turn, n_z)
-        return remote(o_send.at[n, source], o_recv.at[n, source], o_ss.at[n, source], o_rs.at[n, source], {"expert": source})
+    begin_out, pass_out, total_out, close_out = line(o_send, o_recv, o_pass, q_own, o_ss, o_rs, o_ps)
 
     def finish_out(n):
         q_copy(n).wait_recv()
-        both = q_own[lax.rem(n, 2)] + q_recv[n].astype(f32)
-        o_send[n] = both.astype(bf16).reshape(n_z, rows, OUT_COLS)
-        for turn in range(1, n_z):
-            o_copy(n, turn).start()
+        q_own[n] += q_recv[n].astype(f32).reshape(n_z, rows, OUT_COLS)
+        begin_out(n)
 
     out_chunks = w2.shape[1] // OUT_COLS
     for e in range(experts):
@@ -221,30 +247,30 @@
         columns = pl.ds(pl.multiple_of(n * OUT_COLS, OUT_COLS), OUT_COLS)
         q_send[n] = jnp.dot(wide[0], w2[:, columns], preferred_element_type=f32).astype(bf16)
         q_copy(n).start()
-        q_own[lax.rem(n, 2)] = jnp.dot(wide[1], w2[:, columns], preferred_element_type=f32)
+        q_own[n] = jnp.dot(wide[1], w2[:, columns], preferred_element_type=f32).reshape(n_z, rows, OUT_COLS)
 
         @pl.when(n > 0)
         def _():
             finish_out(n - 1)
+
+        @pl.when(n > 1)
+        def _():
+            pass_out(n - 2)
         return carry
 
     lax.fori_loop(0, out_chunks, step_out, 0)
     finish_out(out_chunks - 1)
+    for n in range(max(out_chunks - 2, 0), out_chunks):
+        pass_out(n)
 
     for n in range(out_chunks):
-        total = o_send[n, z].astype(f32)
-        for turn in range(1, n_z):
-            o_arrival(n, turn).wait_recv()
-        for turn in range(1, n_z):
-            total = total + o_recv[n, shift(z, turn, n_z)].astype(f32)
-        out[:, n * OUT_COLS:(n + 1) * OUT_COLS] = total.astype(bf16)
+        out[:, n * OUT_COLS:(n + 1) * OUT_COLS] = total_out(n).astype(bf16)
 
     for turn in range(1, blocks):
         route_copy(turn).wait_send()
     for n in range(chunks):
         sib_copy(n).wait_send()
-        for turn in range(1, n_z):
-            z_copy(n, turn).wait_send()
+        close(n)
     for jj in range(per_plane):
         for xx in range(n_x):
             @pl.when(jnp.logical_not(is_me(jj, xx)))
@@ -252,8 +278,7 @@
                 h_copy(jj, xx).wait_send()
     for n in range(out_chunks):
         q_copy(n).wait_send()
-        for turn in range(1, n_z):
-            o_copy(n, turn).wait_send()
+        close_out(n)
 
 
 def fused(sizes, xs, route, w1, w2):
@@ -277,24 +302,26 @@
             vmem((2, n_z * slots, experts * d_loc), bf16),
             vmem((chunks, n_z * slots, 2 * LANE), bf16),
             vmem((chunks, n_z * slots, 2 * LANE), bf16),
-            vmem((2, n_z * slots, 2 * LANE), f32),
+            vmem((chunks, n_z, slots, 2 * LANE), f32),
             vmem((chunks, n_z, slots, 2 * LANE), bf16),
-            vmem((chunks, n_z, slots, 2 * LANE), bf16),
+            vmem((chunks, 2, slots, 2 * LANE), bf16),
+            vmem((chunks, 2, slots, 2 * LANE), bf16),
             vmem((chunks, slots, LANE), bf16),
             vmem((n_dev, span, slots, LANE), bf16),
             vmem((2, n_z * rows, experts * span * LANE), bf16),
             vmem((out_chunks, n_z * rows, OUT_COLS), bf16),
             vmem((out_chunks, n_z * rows, OUT_COLS), bf16),
-            vmem((2, n_z * rows, OUT_COLS), f32),
+            vmem((out_chunks, n_z, rows, OUT_COLS), f32),
             vmem((out_chunks, n_z, rows, OUT_COLS), bf16),
-            vmem((out_chunks, n_z, rows, OUT_COLS), bf16),
+            vmem((out_chunks, 2, rows, OUT_COLS), bf16),
+            vmem((out_chunks, 2, rows, OUT_COLS), bf16),
             dma((chunks, experts, 2)), dma((experts,)),
             dma((n_dev,)), dma((n_dev,)),
             dma((chunks,)), dma((chunks,)),
-            dma((chunks, n_z)), dma((chunks, n_z)),
+            dma((chunks, n_z)), dma((chunks, 2)), dma((chunks, 2)),
             dma((per_plane, n_x)), dma((n_dev,)),
             dma((out_chunks,)), dma((out_chunks,)),
-            dma((out_chunks, n_z)), dma((out_chunks, n_z)),
+            dma((out_chunks, n_z)), dma((out_chunks, 2)), dma((out_chunks, 2)),
         ],
         compiler_params=pltpu.CompilerParams(
             collective_id=0, has_side_effects=True, vmem_limit_bytes=58 * 1024 * 1024),
@@ -302,7 +329,7 @@
 
 
 def kernel_sizes(n_z, n_c, n_x, top, experts, rows, d_loc, f_loc, units, cols):
-    if n_c != 2 or units % LANE or cols % OUT_COLS or rows % 16 or (n_z * n_c) % n_x:
+    if n_z != 4 or n_c != 2 or units % LANE or cols % OUT_COLS or rows % 16 or (n_z * n_c) % n_x:
         return None
     spans = [-(-((j + 1) * f_loc) // LANE) - j * f_loc // LANE for j in range(n_z * n_c // n_x)]
     span = max(spans)

time: 128 us -> 122 us (0.953)
  Pallas kernels: 99.5 us -> 93.3 us
    pallas_call x1, Pallas kernels: 99.5 us -> 93.3 us  [fused(): pl.pallas_call(functools.partial(kernel, sizes), out_shape=jax.ShapeDtype...]
  transfers between devices with their start and end apart: 1 -> 1, of which waited for: 0 -> 0; matrix products, arithmetic and copies ran while one was open for 13% -> 14% of each run, Pallas kernels for 0% -> 0%
where the time goes in v4:
time: 122 us
  Pallas kernels  93.3 us (76%)
  matrix products  15 us (12%)
  starting transfers between devices  6.33 us (5%)
  local copies, waits for them, and re-layouts  5.37 us (4%)
  other arithmetic  1.52 us (1%)
    pallas_call x1, Pallas kernels, fused(): pl.pallas_call(functools.partial(kernel, sizes), out_shape=jax.ShapeDtype...  93.3 us
    dot_general x4, matrix products, take(): jnp.tensordot(scales, onehot, axes=([axis], [1]), precision=lax.Precision...  15 us
    all_to_all x1, starting transfers between devices, body(): xs = lax.all_to_all(xs, ROW_AXES, split_axis=0, concat_axis=0, tiled=True)  6.33 us
    unnamed x8, local copies, waits for them, and re-layouts  3.7 us
  transfers between devices with their start and end apart: 1, of which 0 were waited for; matrix products, arithmetic and copies ran while one was open for 14% of the time, Pallas kernels for 0%

profile of v4, /device:TPU:0, one launch (start us, length us, event | category | flops | bytes accessed | tf_op | source)
XLA Modules:
  0.0 121.6 jit_solution(5284655908108811860)
XLA Ops:
  0.0 0.0 copy-start
  0.0 1.2 %copy.17 = bf16[8,8,8,512]{3,2,1,0:T(8,128)(2,1)S(1)} copy(bf16[8,8,8,512]{3,1,2,0:T(8,128)(2,1)} %bitcast.36) | data formatting | bytes 1048576
  1.2 1.0 copy.24
  2.2 6.3 %all-to-all-start = ((bf16[8,64,512]{2,1,0:T(8,128)(2,1)}), bf16[8,64,512]{2,1,0:T(8,128)(2,1)S(1)}, u32[]{:S(2)}, u32[]{:S(2)}) async-start(bf16[8,64,512]{2,1,0:T(8,128)(2,1)} %bitcast.33), calls=%async_computation | async-start | bytes 1048576 | tf_op jit(solution)/shard_map/all_to_all | solution.py:440
  8.5 0.8 fusion.24
  9.3 0.7 convert_element_type.21
  10.0 0.1 copy.11
  10.1 0.0 copy-start.1
  10.2 0.6 pad.4.my_route
  10.8 0.0 copy-done
  10.8 0.4 convolution_bitcast_fusion
  11.2 1.5 %convolution_bitcast_fusion.1 = f32[4,192,32]{1,2,0:T(8,128)S(1)} fusion(s32[192]{0:T(256)S(1)} %and_select_fusion, f32[4,12,32]{2,0,1:T(4,128)} %param.13), kind=kOutput, calls=%fused_computation.4 | convolution fusion | flops 3541248 | bytes 105216 | tf_op jit(solution)/shard_map/dot_general | solution.py:423
  12.7 5.7 %multiply_convert_fusion.1.w2_in = bf16[4,192,2048]{2,1,0:T(8,128)(2,1)} fusion(bf16[4,192,2048]{2,1,0:T(8,128)(2,1)} %param.12, f32[4,192,32]{1,2,0:T(8,128)S(1)} %convolution_bitcast_fusion.1, s32[2048]{0:T(1024)S(1)} %add_select_fusion), kind=kOutput, calls=%fused_computation.2 | convolution fusion | flops 608763904 | bytes 6397952 | tf_op jit(solution)/shard_map/dot_general | solution.py:423
  18.4 0.0 copy-done.1
  18.4 7.4 %fusion.w1_in = bf16[4,2,512,768]{3,2,1,0:T(8,128)(2,1)} fusion(bf16[4,512,2,768]{3,2,1,0:T(2,128)(2,1)S(1)} %copy-done.1, f32[4,512,2,12]{1,3,2,0:T(8,128)S(1)} %convolution_bitcast_fusion, s32[768]{0:T(1024)S(1)} %add_select_fusion.1), kind=kOutput, calls=%fused_computation.1 | convolution fusion | flops 462431232 | bytes 12782592 | tf_op jit(solution)/shard_map/dot_general | solution.py:423
  25.8 0.0 all-to-all-done.xs
  25.8 0.0 copy-start.2
  25.8 0.8 copy-done.2
  26.6 93.3 %shard_map.73 = bf16[64,2048]{1,0:T(8,128)(2,1)} custom-call(bf16[8,64,512]{2,1,0:T(8,128)(2,1)} %copy-done.2, f32[64,128]{1,0:T(8,128)} %pad.4.my_route, bf16[4,2,512,768]{3,2,1,0:T(8,128)(2,1)} %fusion.w1_in, bf16[4,192,2048]{2,1,0:T(8,128)(2,1)} %multiply_convert_fusion.1.w2_in), custom_call_target="tpu_custom_call" | custom-call | tf_op jit(solution)/shard_map/pallas_call | solution.py:293
  120.0 1.7 %copy.26 = bf16[4,16,2048]{2,1,0:T(8,128)(2,1)} copy(bf16[4,16,2048]{2,1,0:T(8,128)(2,1)} %bitcast.35) | data formatting | bytes 524288
  (5 shorter events, 0.1 us)
Async XLA Ops:
  0.0 10.8 %copy-start = (f32[4,32,2,12]{1,2,3,0:T(2,128)S(1)}, f32[4,32,2,12]{1,2,3,0:T(2,128)}, u32[]{:S(2)}) copy-start(f32[4,32,2,12]{1,2,3,0:T(2,128)} %param.11) | copy-start | bytes 36868
  2.2 23.6 %all-to-all-start = ((bf16[8,64,512]{2,1,0:T(8,128)(2,1)}), bf16[8,64,512]{2,1,0:T(8,128)(2,1)S(1)}, u32[]{:S(2)}, u32[]{:S(2)}) async-start(bf16[8,64,512]{2,1,0:T(8,128)(2,1)} %bitcast.33), calls=%async_computation | async-start | bytes 1048576 | tf_op jit(solution)/shard_map/all_to_all | solution.py:440
  10.1 8.3 %copy-start.1 = (bf16[4,512,2,768]{3,2,1,0:T(2,128)(2,1)S(1)}, bf16[4,512,2,768]{3,2,1,0:T(2,128)(2,1)}, u32[]{:S(2)}) copy-start(bf16[4,512,2,768]{3,2,1,0:T(2,128)(2,1)} %param.10) | copy-start | bytes 18874372
  25.8 0.8 copy-start.2

commit v5 on v4

--- a/solution.py
+++ b/solution.py
@@ -16,9 +16,9 @@
     return lax.rem(index + by, count)
 
 
-def kernel(sizes, xs, my_route, w1_in, w2_in, out, route, w1, w2, xm, s_send, s_recv, own, z_send, z_recv, z_pass, hid, h_recv,
+def kernel(sizes, xs, my_route, s2, w1_in, w2_in, out, route, w1, w2, xm, s_send, s_recv, own, z_send, z_recv, z_pass, hid, h_recv,
            wide, q_send, q_recv, q_own, o_send, o_recv, o_pass,
-           w1_s, w2_s, r_ss, r_rs, s_ss, s_rs, z_ss, z_rs, z_ps, h_ss, h_rs, q_ss, q_rs, o_ss, o_rs, o_ps):
+           w1_s, w2_s, r_ss, r_rs, s_ss, s_rs, z_ss, z_rs, z_ps, h_ss, h_fs, h_rs, q_ss, q_rs, o_ss, o_rs, o_ps):
     n_z, n_x, top, experts, rows, d_loc, f_loc, span = sizes
     n_c = 2
     f32, bf16 = jnp.float32, jnp.bfloat16
@@ -157,6 +157,14 @@
         own[n] += s_recv[n].astype(f32).reshape(n_z, slots, 2 * LANE)
         begin(n)
 
+    def scale_down(e):
+        w2_copy(e).wait()
+        band = pl.ds(pl.multiple_of(e * depth + offset, 16), f_loc)
+        scales = s2[e]
+        for b in range(w2.shape[1] // LANE):
+            columns = slice(b * LANE, (b + 1) * LANE)
+            w2[band, columns] = (w2[band, columns].astype(f32) * scales[:, b:b + 1]).astype(bf16)
+
     def step(n, carry):
         for e in range(experts):
             for g in range(2):
@@ -172,6 +180,10 @@
         @pl.when(n > 1)
         def _():
             pass_on(n - 2)
+
+        @pl.when(n < experts)
+        def _():
+            scale_down(n)
         return carry
 
     lax.fori_loop(0, chunks, step, 0)
@@ -181,14 +193,19 @@
 
     mine = route[me]
 
-    def h_copy(jj, xx):
+    source_x = me // per_plane
+
+    def h_copy(jj):
         owner = per_plane * x + jj
         first = jj * f_loc // LANE
-        return remote(hid.at[pl.ds(first, span)], h_recv.at[me], h_ss.at[jj, xx], h_rs.at[me],
-                      {"expert": owner // n_c, "learner": owner % n_c, "replica": xx})
-
-    def is_me(jj, xx):
-        return (per_plane * x + jj == me) & (x == xx)
+        return remote(hid.at[pl.ds(first, span)], h_recv.at[me], h_ss.at[jj], h_rs.at[me],
+                      {"expert": owner // n_c, "learner": owner % n_c})
+
+    def h_forward(p):
+        return remote(h_recv.at[p], h_recv.at[p], h_fs.at[p], h_rs.at[p], {"replica": 1 - x})
+
+    def is_me(jj):
+        return per_plane * x + jj == me
 
     for n in range(chunks):
         total = total_of(n)
@@ -201,21 +218,26 @@
             first = jj * f_loc // LANE
             if first + span - 1 != n:
                 continue
-            for xx in range(n_x):
-                @pl.when(jnp.logical_not(is_me(jj, xx)))
-                def _(jj=jj, xx=xx):
-                    h_copy(jj, xx).start()
-
-                @pl.when(is_me(jj, xx))
-                def _(first=first):
-                    h_recv[me] = hid[first:first + span]
-
-    source_x = me // per_plane
-    for p in range(n_z * n_c):
-        @pl.when(jnp.logical_not((p == me) & (source_x == x)))
-        def _(p=p):
-            remote(hid.at[pl.ds(0, span)], h_recv.at[p], h_ss.at[0, 0], h_rs.at[p],
-                   {"expert": p // n_c, "learner": p % n_c, "replica": source_x}).wait_recv()
+            @pl.when(jnp.logical_not(is_me(jj)))
+            def _(jj=jj):
+                h_copy(jj).start()
+
+            @pl.when(is_me(jj))
+            def _(first=first):
+                h_recv[me] = hid[first:first + span]
+
+    @pl.when(source_x == x)
+    def _():
+        h_forward(me).start()
+        for turn in range(1, blocks):
+            p = shift(me, turn, blocks)
+            h_forward(p).wait_recv()
+            h_forward(p).start()
+
+    @pl.when(source_x != x)
+    def _():
+        for p in range(blocks):
+            h_forward(p).wait_recv()
 
     for half in range(2):
         for zz in range(n_z):
@@ -240,8 +262,8 @@
         begin_out(n)
 
     out_chunks = w2.shape[1] // OUT_COLS
-    for e in range(experts):
-        w2_copy(e).wait()
+    for e in range(chunks, experts):
+        scale_down(e)
 
     def step_out(n, carry):
         columns = pl.ds(pl.multiple_of(n * OUT_COLS, OUT_COLS), OUT_COLS)
@@ -272,16 +294,20 @@
         sib_copy(n).wait_send()
         close(n)
     for jj in range(per_plane):
-        for xx in range(n_x):
-            @pl.when(jnp.logical_not(is_me(jj, xx)))
-            def _(jj=jj, xx=xx):
-                h_copy(jj, xx).wait_send()
+        @pl.when(jnp.logical_not(is_me(jj)))
+        def _(jj=jj):
+            h_copy(jj).wait_send()
+
+    @pl.when(source_x == x)
+    def _():
+        for p in range(blocks):
+            h_forward(p).wait_send()
     for n in range(out_chunks):
         q_copy(n).wait_send()
         close_out(n)
 
 
-def fused(sizes, xs, route, w1, w2):
+def fused(sizes, xs, route, s2, w1, w2):
     n_z, n_x, top, experts, rows, d_loc, f_loc, span = sizes
     n_dev = 2 * n_z
     chunks, cols = w1.shape[3] // LANE, w2.shape[2]
@@ -293,7 +319,7 @@
     return pl.pallas_call(
         functools.partial(kernel, sizes),
         out_shape=jax.ShapeDtypeStruct((rows, cols), bf16),
-        in_specs=[pl.BlockSpec(memory_space=pltpu.VMEM)] * 2 + [pl.BlockSpec(memory_space=pl.ANY)] * 2,
+        in_specs=[pl.BlockSpec(memory_space=pltpu.VMEM)] * 3 + [pl.BlockSpec(memory_space=pl.ANY)] * 2,
         out_specs=pl.BlockSpec(memory_space=pltpu.VMEM),
         scratch_shapes=[
             vmem((n_dev, rows, LANE), f32),
@@ -319,17 +345,17 @@
             dma((n_dev,)), dma((n_dev,)),
             dma((chunks,)), dma((chunks,)),
             dma((chunks, n_z)), dma((chunks, 2)), dma((chunks, 2)),
-            dma((per_plane, n_x)), dma((n_dev,)),
+            dma((per_plane,)), dma((n_dev,)), dma((n_dev,)),
             dma((out_chunks,)), dma((out_chunks,)),
             dma((out_chunks, n_z)), dma((out_chunks, 2)), dma((out_chunks, 2)),
         ],
         compiler_params=pltpu.CompilerParams(
             collective_id=0, has_side_effects=True, vmem_limit_bytes=58 * 1024 * 1024),
-    )(xs, route, w1, w2)
+    )(xs, route, s2, w1, w2)
 
 
 def kernel_sizes(n_z, n_c, n_x, top, experts, rows, d_loc, f_loc, units, cols):
-    if n_z != 4 or n_c != 2 or units % LANE or cols % OUT_COLS or rows % 16 or (n_z * n_c) % n_x:
+    if n_x != 2 or n_z != 4 or n_c != 2 or units % LANE or cols % OUT_COLS or rows % 16 or (n_z * n_c) % n_x:
         return None
     spans = [-(-((j + 1) * f_loc) // LANE) - j * f_loc // LANE for j in range(n_z * n_c // n_x)]
     span = max(spans)
@@ -425,21 +451,24 @@
 
     s1 = take(take(gate_up_scales, 1, me * d_loc, d_loc), 3, x * units, units)
     w1 = (gate_up_tiles.astype(f32) * s1).astype(bf16)
-    s2 = take(take(down_scales, 1, me * f_loc, f_loc), 2, x * cols, cols)
-    w2 = (down_tiles.astype(f32) * s2).astype(bf16)
+    s2 = take(down_scales, 1, me * f_loc, f_loc)
 
 
     rows = steps * rows_dev
     share = gates / jnp.sum(gates, axis=2, keepdims=True)
     route = jnp.concatenate([expert_ids.astype(f32), share], axis=2).reshape(1, rows, 2 * top)
     sizes = kernel_sizes(n_z, n_c, n_x, top, experts, rows, d_loc, f_loc, units, cols)
-    if sizes is None:
+    if sizes is None or tile != LANE:
+        s2 = take(s2, 2, x * cols, cols)
+        w2 = (down_tiles.astype(f32) * s2).astype(bf16)
         route = lax.all_gather(route, ROW_AXES, axis=0, tiled=True)
         return plain(tokens, route, w1, w2, n_x)
     xs = jnp.swapaxes(tokens.reshape(rows, n_dev, d_loc), 0, 1)
     xs = lax.all_to_all(xs, ROW_AXES, split_axis=0, concat_axis=0, tiled=True)
     route = jnp.pad(route[0], ((0, 0), (0, LANE - 2 * top)))
-    out = fused(sizes, xs, route, jnp.swapaxes(w1, 1, 2), w2)
+    s2 = lax.dynamic_slice_in_dim(s2, x * (cols // LANE), cols // LANE, 2)
+    s2 = jnp.pad(s2, ((0, 0), (0, 0), (0, LANE - cols // LANE)))
+    out = fused(sizes, xs, route, s2, jnp.swapaxes(w1, 1, 2), down_tiles)
     return out.reshape(steps, rows_dev, cols)
 
 

time: 122 us -> 118 us (0.967)
  matrix products: 15 us -> 11.2 us
  Pallas kernels: 93.3 us -> 90.8 us
    dot_general x4 -> x3, matrix products: 15 us -> 11.2 us  [take(): jnp.tensordot(scales, onehot, axes=([axis], [1]), precision=lax.Precision...]
    pallas_call x1, Pallas kernels: 93.3 us -> 90.8 us  [fused(): pl.pallas_call(functools.partial(kernel, sizes), out_shape=jax.ShapeDtype...]
    unnamed x8 -> x6, local copies, waits for them, and re-layouts: 3.7 us -> 3.69 us
  transfers between devices with their start and end apart: 1 -> 1, of which waited for: 0 -> 1; matrix products, arithmetic and copies ran while one was open for 14% -> 12% of each run, Pallas kernels for 0% -> 0%
where the time goes in v5:
time: 118 us; the launch traced here: 117 us
  Pallas kernels  90.8 us (77%)
  matrix products  11.2 us (9%)
  starting transfers between devices  6.33 us (5%)
  local copies, waits for them, and re-layouts  6.32 us (5%)
  other arithmetic  1.52 us (1%)
    pallas_call x1, Pallas kernels, fused(): pl.pallas_call(functools.partial(kernel, sizes), out_shape=jax.ShapeDtype...  90.8 us
    dot_general x3, matrix products, take(): jnp.tensordot(scales, onehot, axes=([axis], [1]), precision=lax.Precision...  11.2 us
    all_to_all x1, starting transfers between devices, body(): xs = lax.all_to_all(xs, ROW_AXES, split_axis=0, concat_axis=0, tiled=True)  6.33 us
    unnamed x6, local copies, waits for them, and re-layouts  3.69 us
  transfers between devices with their start and end apart: 1, of which 1 were waited for; matrix products, arithmetic and copies ran while one was open for 12% of the time, Pallas kernels for 0%

profile of v5, /device:TPU:0, one launch (start us, length us, event | category | flops | bytes accessed | tf_op | source)
XLA Modules:
  0.0 117.2 jit_solution(15319689076759405013)
XLA Ops:
  0.0 0.0 copy-start
  0.0 1.2 %copy.21 = bf16[8,8,8,512]{3,2,1,0:T(8,128)(2,1)S(1)} copy(bf16[8,8,8,512]{3,1,2,0:T(8,128)(2,1)} %bitcast.32) | data formatting | bytes 1048576
  1.2 1.0 copy.28
  2.2 6.3 %all-to-all-start = ((bf16[8,64,512]{2,1,0:T(8,128)(2,1)}), bf16[8,64,512]{2,1,0:T(8,128)(2,1)S(1)}, u32[]{:S(2)}, u32[]{:S(2)}) async-start(bf16[8,64,512]{2,1,0:T(8,128)(2,1)} %bitcast.29), calls=%async_computation | async-start | bytes 1048576 | tf_op jit(solution)/shard_map/all_to_all | solution.py:467
  8.5 0.8 fusion.19
  9.3 0.7 convert_element_type.16
  10.0 1.1 fusion.7
  11.1 0.2 dynamic-slice_bitcast_fusion
  11.3 0.1 copy.13
  11.4 0.6 pad.8.my_route
  12.0 0.8 pad.9.s2
  12.8 0.0 copy-done
  12.9 0.4 convolution_bitcast_fusion
  13.2 9.7 %fusion.w1_in = bf16[4,2,512,768]{3,2,1,0:T(8,128)(2,1)} fusion(bf16[4,512,2,768]{3,2,1,0:T(2,128)(2,1)} %param.10, f32[4,512,2,12]{1,3,2,0:T(8,128)S(1)} %convolution_bitcast_fusion, s32[768]{0:T(1024)S(1)} %add_select_fusion), kind=kOutput, calls=%fused_computation.1 | convolution fusion | flops 462431232 | bytes 12782592 | tf_op jit(solution)/shard_map/dot_general | solution.py:449
  22.9 0.9 all-to-all-done.xs
  23.9 0.0 copy-start.1
  23.9 0.8 copy-done.1
  24.7 90.8 %shard_map.73 = bf16[64,2048]{1,0:T(8,128)(2,1)} custom-call(bf16[8,64,512]{2,1,0:T(8,128)(2,1)} %copy-done.1, f32[64,128]{1,0:T(8,128)} %pad.8.my_route, f32[4,192,128]{2,1,0:T(8,128)} %pad.9.s2, bf16[4,2,512,768]{3,2,1,0:T(8,128)(2,1)} %fusion.w1_in, bf16[4,192,2048]{2,1,0:T(8,128)(2,1)} %w2_in.1), custom_call_target="tpu_custom_call" | custom-call | tf_op jit(solution)/shard_map/pallas_call | solution.py:319
  115.5 1.7 %copy.30 = bf16[4,16,2048]{2,1,0:T(8,128)(2,1)} copy(bf16[4,16,2048]{2,1,0:T(8,128)(2,1)} %bitcast.31) | data formatting | bytes 524288
  (4 shorter events, 0.0 us)
Async XLA Ops:
  0.0 12.8 %copy-start = (f32[4,32,2,12]{1,2,3,0:T(2,128)S(1)}, f32[4,32,2,12]{1,2,3,0:T(2,128)}, u32[]{:S(2)}) copy-start(f32[4,32,2,12]{1,2,3,0:T(2,128)} %param.11) | copy-start | bytes 36868
  2.2 21.7 %all-to-all-start = ((bf16[8,64,512]{2,1,0:T(8,128)(2,1)}), bf16[8,64,512]{2,1,0:T(8,128)(2,1)S(1)}, u32[]{:S(2)}, u32[]{:S(2)}) async-start(bf16[8,64,512]{2,1,0:T(8,128)(2,1)} %bitcast.29), calls=%async_computation | async-start | bytes 1048576 | tf_op jit(solution)/shard_map/all_to_all | solution.py:467
  23.9 0.8 copy-start.1

commit v6 on v5

--- a/solution.py
+++ b/solution.py
@@ -199,13 +199,19 @@
         owner = per_plane * x + jj
         first = jj * f_loc // LANE
         return remote(hid.at[pl.ds(first, span)], h_recv.at[me], h_ss.at[jj], h_rs.at[me],
-                      {"expert": owner // n_c, "learner": owner % n_c})
+                      {"expert": owner // n_c, "learner": owner % n_c,
+                       "replica": jnp.where(c == 0, x, 1 - x)})
 
     def h_forward(p):
         return remote(h_recv.at[p], h_recv.at[p], h_fs.at[p], h_rs.at[p], {"replica": 1 - x})
 
     def is_me(jj):
-        return per_plane * x + jj == me
+        return (per_plane * x + jj == me) & (c == 0)
+
+    kind = jnp.where(source_x == x, 0, 1)
+
+    def landed(turn):
+        return shift(z, turn, n_z) * n_c + kind
 
     for n in range(chunks):
         total = total_of(n)
@@ -226,18 +232,16 @@
             def _(first=first):
                 h_recv[me] = hid[first:first + span]
 
-    @pl.when(source_x == x)
-    def _():
-        h_forward(me).start()
-        for turn in range(1, blocks):
-            p = shift(me, turn, blocks)
+    for turn in range(n_z):
+        p = landed(turn)
+
+        @pl.when(jnp.logical_not((p == me) & (kind == 0)))
+        def _(p=p):
             h_forward(p).wait_recv()
-            h_forward(p).start()
-
-    @pl.when(source_x != x)
-    def _():
-        for p in range(blocks):
-            h_forward(p).wait_recv()
+
+        h_forward(p).start()
+    for turn in range(n_z):
+        h_forward(shift(z, turn, n_z) * n_c + 1 - kind).wait_recv()
 
     for half in range(2):
         for zz in range(n_z):
@@ -298,10 +302,8 @@
         def _(jj=jj):
             h_copy(jj).wait_send()
 
-    @pl.when(source_x == x)
-    def _():
-        for p in range(blocks):
-            h_forward(p).wait_send()
+    for turn in range(n_z):
+        h_forward(landed(turn)).wait_send()
     for n in range(out_chunks):
         q_copy(n).wait_send()
         close_out(n)

time: 118 us -> 115 us (0.975)
  Pallas kernels: 90.8 us -> 87.8 us
    pallas_call x1, Pallas kernels: 90.8 us -> 87.8 us  [fused(): pl.pallas_call(functools.partial(kernel, sizes), out_shape=jax.ShapeDtype...]
  transfers between devices with their start and end apart: 1 -> 1, of which waited for: 1 -> 1; matrix products, arithmetic and copies ran while one was open for 12% -> 13% of each run, Pallas kernels for 0% -> 0%
where the time goes in v6:
time: 115 us; the launch traced here: 114 us
  Pallas kernels  87.8 us (76%)
  matrix products  11.2 us (10%)
  starting transfers between devices  6.33 us (6%)
  local copies, waits for them, and re-layouts  6.32 us (5%)
  other arithmetic  1.52 us (1%)
    pallas_call x1, Pallas kernels, fused(): pl.pallas_call(functools.partial(kernel, sizes), out_shape=jax.ShapeDtype...  87.8 us
    dot_general x3, matrix products, take(): jnp.tensordot(scales, onehot, axes=([axis], [1]), precision=lax.Precision...  11.2 us
    all_to_all x1, starting transfers between devices, body(): xs = lax.all_to_all(xs, ROW_AXES, split_axis=0, concat_axis=0, tiled=True)  6.33 us
    unnamed x6, local copies, waits for them, and re-layouts  3.69 us
  transfers between devices with their start and end apart: 1, of which 1 were waited for; matrix products, arithmetic and copies ran while one was open for 13% of the time, Pallas kernels for 0%

profile of v6, /device:TPU:0, one launch (start us, length us, event | category | flops | bytes accessed | tf_op | source)
XLA Modules:
  0.0 114.1 jit_solution(7621184971502800065)
XLA Ops:
  0.0 0.0 copy-start
  0.0 1.2 %copy.21 = bf16[8,8,8,512]{3,2,1,0:T(8,128)(2,1)S(1)} copy(bf16[8,8,8,512]{3,1,2,0:T(8,128)(2,1)} %bitcast.32) | data formatting | bytes 1048576
  1.2 1.0 copy.28
  2.2 6.3 %all-to-all-start = ((bf16[8,64,512]{2,1,0:T(8,128)(2,1)}), bf16[8,64,512]{2,1,0:T(8,128)(2,1)S(1)}, u32[]{:S(2)}, u32[]{:S(2)}) async-start(bf16[8,64,512]{2,1,0:T(8,128)(2,1)} %bitcast.29), calls=%async_computation | async-start | bytes 1048576 | tf_op jit(solution)/shard_map/all_to_all | solution.py:469
  8.5 0.8 fusion.19
  9.3 0.7 convert_element_type.16
  10.0 1.1 fusion.7
  11.1 0.2 dynamic-slice_bitcast_fusion
  11.3 0.1 copy.13
  11.4 0.6 pad.8.my_route
  12.0 0.8 pad.9.s2
  12.8 0.0 copy-done
  12.9 0.4 convolution_bitcast_fusion
  13.2 9.7 %fusion.w1_in = bf16[4,2,512,768]{3,2,1,0:T(8,128)(2,1)} fusion(bf16[4,512,2,768]{3,2,1,0:T(2,128)(2,1)} %param.10, f32[4,512,2,12]{1,3,2,0:T(8,128)S(1)} %convolution_bitcast_fusion, s32[768]{0:T(1024)S(1)} %add_select_fusion), kind=kOutput, calls=%fused_computation.1 | convolution fusion | flops 462431232 | bytes 12782592 | tf_op jit(solution)/shard_map/dot_general | solution.py:451
  22.9 0.9 all-to-all-done.xs
  23.9 0.0 copy-start.1
  23.9 0.8 copy-done.1
  24.7 87.8 %shard_map.73 = bf16[64,2048]{1,0:T(8,128)(2,1)} custom-call(bf16[8,64,512]{2,1,0:T(8,128)(2,1)} %copy-done.1, f32[64,128]{1,0:T(8,128)} %pad.8.my_route, f32[4,192,128]{2,1,0:T(8,128)} %pad.9.s2, bf16[4,2,512,768]{3,2,1,0:T(8,128)(2,1)} %fusion.w1_in, bf16[4,192,2048]{2,1,0:T(8,128)(2,1)} %w2_in.1), custom_call_target="tpu_custom_call" | custom-call | tf_op jit(solution)/shard_map/pallas_call | solution.py:321
  112.5 1.7 %copy.30 = bf16[4,16,2048]{2,1,0:T(8,128)(2,1)} copy(bf16[4,16,2048]{2,1,0:T(8,128)(2,1)} %bitcast.31) | data formatting | bytes 524288
  (4 shorter events, 0.0 us)
Async XLA Ops:
  0.0 12.8 %copy-start = (f32[4,32,2,12]{1,2,3,0:T(2,128)S(1)}, f32[4,32,2,12]{1,2,3,0:T(2,128)}, u32[]{:S(2)}) copy-start(f32[4,32,2,12]{1,2,3,0:T(2,128)} %param.11) | copy-start | bytes 36868
  2.2 21.7 %all-to-all-start = ((bf16[8,64,512]{2,1,0:T(8,128)(2,1)}), bf16[8,64,512]{2,1,0:T(8,128)(2,1)S(1)}, u32[]{:S(2)}, u32[]{:S(2)}) async-start(bf16[8,64,512]{2,1,0:T(8,128)(2,1)} %bitcast.29), calls=%async_computation | async-start | bytes 1048576 | tf_op jit(solution)/shard_map/all_to_all | solution.py:469
  23.9 0.8 copy-start.1

commit v7 on v6

--- a/solution.py
+++ b/solution.py
@@ -9,7 +9,7 @@
 
 ROW_AXES = ("expert", "learner")
 LANE = 128
-OUT_COLS = 512
+OUT_COLS = 256
 
 
 def shift(index, by, count):

time: 115 us -> 115 us (level)
  no operation moved by 1% of the time
where the time goes in v7:
time: 115 us
  Pallas kernels  88.5 us (77%)
  matrix products  11.2 us (10%)
  starting transfers between devices  6.33 us (6%)
  local copies, waits for them, and re-layouts  6.32 us (5%)
  other arithmetic  1.52 us (1%)
    pallas_call x1, Pallas kernels, fused(): pl.pallas_call(functools.partial(kernel, sizes), out_shape=jax.ShapeDtype...  88.5 us
    dot_general x3, matrix products, take(): jnp.tensordot(scales, onehot, axes=([axis], [1]), precision=lax.Precision...  11.2 us
    all_to_all x1, starting transfers between devices, body(): xs = lax.all_to_all(xs, ROW_AXES, split_axis=0, concat_axis=0, tiled=True)  6.33 us
    unnamed x6, local copies, waits for them, and re-layouts  3.69 us
  transfers between devices with their start and end apart: 1, of which 1 were waited for; matrix products, arithmetic and copies ran while one was open for 13% of the time, Pallas kernels for 0%

profile of v7, /device:TPU:0, one launch (start us, length us, event | category | flops | bytes accessed | tf_op | source)
XLA Modules:
  0.0 114.8 jit_solution(13538740858399935617)
XLA Ops:
  0.0 0.0 copy-start
  0.0 1.2 %copy.21 = bf16[8,8,8,512]{3,2,1,0:T(8,128)(2,1)S(1)} copy(bf16[8,8,8,512]{3,1,2,0:T(8,128)(2,1)} %bitcast.32) | data formatting | bytes 1048576
  1.2 1.0 copy.28
  2.2 6.3 %all-to-all-start = ((bf16[8,64,512]{2,1,0:T(8,128)(2,1)}), bf16[8,64,512]{2,1,0:T(8,128)(2,1)S(1)}, u32[]{:S(2)}, u32[]{:S(2)}) async-start(bf16[8,64,512]{2,1,0:T(8,128)(2,1)} %bitcast.29), calls=%async_computation | async-start | bytes 1048576 | tf_op jit(solution)/shard_map/all_to_all | solution.py:469
  8.5 0.8 fusion.19
  9.3 0.7 convert_element_type.16
  10.0 1.1 fusion.7
  11.1 0.2 dynamic-slice_bitcast_fusion
  11.3 0.1 copy.13
  11.4 0.6 pad.8.my_route
  12.0 0.8 pad.9.s2
  12.8 0.0 copy-done
  12.9 0.4 convolution_bitcast_fusion
  13.2 9.7 %fusion.w1_in = bf16[4,2,512,768]{3,2,1,0:T(8,128)(2,1)} fusion(bf16[4,512,2,768]{3,2,1,0:T(2,128)(2,1)} %param.10, f32[4,512,2,12]{1,3,2,0:T(8,128)S(1)} %convolution_bitcast_fusion, s32[768]{0:T(1024)S(1)} %add_select_fusion), kind=kOutput, calls=%fused_computation.1 | convolution fusion | flops 462431232 | bytes 12782592 | tf_op jit(solution)/shard_map/dot_general | solution.py:451
  22.9 0.9 all-to-all-done.xs
  23.9 0.0 copy-start.1
  23.9 0.8 copy-done.1
  24.7 88.5 %shard_map.73 = bf16[64,2048]{1,0:T(8,128)(2,1)} custom-call(bf16[8,64,512]{2,1,0:T(8,128)(2,1)} %copy-done.1, f32[64,128]{1,0:T(8,128)} %pad.8.my_route, f32[4,192,128]{2,1,0:T(8,128)} %pad.9.s2, bf16[4,2,512,768]{3,2,1,0:T(8,128)(2,1)} %fusion.w1_in, bf16[4,192,2048]{2,1,0:T(8,128)(2,1)} %w2_in.1), custom_call_target="tpu_custom_call" | custom-call | tf_op jit(solution)/shard_map/pallas_call | solution.py:321
  113.1 1.7 %copy.30 = bf16[4,16,2048]{2,1,0:T(8,128)(2,1)} copy(bf16[4,16,2048]{2,1,0:T(8,128)(2,1)} %bitcast.31) | data formatting | bytes 524288
  (4 shorter events, 0.0 us)
Async XLA Ops:
  0.0 12.8 %copy-start = (f32[4,32,2,12]{1,2,3,0:T(2,128)S(1)}, f32[4,32,2,12]{1,2,3,0:T(2,128)}, u32[]{:S(2)}) copy-start(f32[4,32,2,12]{1,2,3,0:T(2,128)} %param.11) | copy-start | bytes 36868
  2.2 21.7 %all-to-all-start = ((bf16[8,64,512]{2,1,0:T(8,128)(2,1)}), bf16[8,64,512]{2,1,0:T(8,128)(2,1)S(1)}, u32[]{:S(2)}, u32[]{:S(2)}) async-start(bf16[8,64,512]{2,1,0:T(8,128)(2,1)} %bitcast.29), calls=%async_computation | async-start | bytes 1048576 | tf_op jit(solution)/shard_map/all_to_all | solution.py:469
  23.9 0.8 copy-start.1
